TPU v7x, 256 devices: a whole 4x4x8 slice. The times are simulated.
256 devices in a mesh: ctx: 64 (over z, y, core), head: 4 (over x).
Axes of the slice: x: 4, y: 4, z: 8, core: 2. Of those that a mesh axis runs over, the one named last changes fastest.
Arguments:
- queries: bfloat16 [32768, 2048], P('ctx', 'head'), may hold values from -8 to 8
- keys: bfloat16 [32768, 512], P('ctx', 'head'), may hold values from -12 to 12
- values: bfloat16 [32768, 512], P('ctx', 'head'), may hold values from -6 to 6
- picks: int32 [64, 4, 7], P(None, 'head'), may hold values from 0 to 62, as said below
- out_weight: bfloat16 [2048, 4096], P('head'), may hold values from -0.125 to 0.125
Outputs:
- projected: bfloat16 [32768, 4096], P(('ctx', 'head'))
Inputs may be any that keep to these rules, and one draw needn't show every extreme that they name: `picks`: for query block b and KV head h the first entry is max(b - 1, 0) and every entry lies in 0 to max(b - 1, 0); entries of one list may repeat.
All inputs are finite; a program needn't handle non-finite values.
Results may differ from a plain program's by a relative error of at most 0.018.
Values may be sent and summed in bfloat16 or wider, within the bound.
No kernel may reach another device: no remote copies, remote signals or barrier semaphores. Data moves between devices by JAX's collectives and lax.ppermute only.
A program may use at most 128 MiB of HBM per device.

v0:
```python
import functools
import math

import jax
import jax.numpy as jnp
from jax import lax
from jax.experimental import pallas as pl
from jax.experimental.pallas import tpu as pltpu
from jax.sharding import Mesh
from jax.sharding import PartitionSpec as P

HD = 128
BLOCK = 512
QPK = 4
PICKS = 6
PIECES = 8
ROWS = BLOCK // PIECES
PART = PICKS * ROWS
MEAN_ROWS = 16
MSG = ROWS + MEAN_ROWS
HALF = PIECES // 2 * ROWS
NZ, NY, NC, NX = 8, 4, 2, 4
TILE = BLOCK // NX
STACK = TILE * QPK
SCALE = HD**-0.5 * math.log2(math.e)
WHALF = QPK * HD // NC
FAR = 1e30
MIB = 1 << 20

ANY = pl.BlockSpec(memory_space=pl.ANY)


def params(mib=40):
    return pltpu.CompilerParams(vmem_limit_bytes=mib * MIB)


def cost(flops, nbytes, trans=0):
    return pl.CostEstimate(flops=flops, bytes_accessed=nbytes, transcendentals=trans)


def pack_kernel(k_ref, v_ref, kv_ref, msg_ref):
    k = k_ref[...]
    v = v_ref[...]
    kv_ref[:, :HD] = k
    kv_ref[:, HD:] = v
    mk = jnp.sum(k.astype(jnp.float32), axis=0, keepdims=True) * (1.0 / BLOCK)
    mv = jnp.sum(v.astype(jnp.float32), axis=0, keepdims=True) * (1.0 / BLOCK)
    mean = jnp.concatenate([mk, mv], axis=1).astype(jnp.bfloat16)
    mean = jnp.broadcast_to(mean, (MEAN_ROWS, 2 * HD))
    for r in range(PIECES):
        rows = slice(r * ROWS, (r + 1) * ROWS)
        msg_ref[r, :ROWS, :HD] = k_ref[rows, :]
        msg_ref[r, :ROWS, HD:] = v_ref[rows, :]
        msg_ref[r, ROWS:, :] = mean


def pack(k, v):
    return pl.pallas_call(
        pack_kernel,
        out_shape=[
            jax.ShapeDtypeStruct((BLOCK, 2 * HD), jnp.bfloat16),
            jax.ShapeDtypeStruct((PIECES, MSG, 2 * HD), jnp.bfloat16),
        ],
        compiler_params=params(16),
        cost_estimate=cost(1 << 18, MIB),
        name="pack",
    )(k, v)


def unpack_kernel(msg_ref, a_ref, b_ref):
    row = lax.broadcasted_iota(jnp.int32, (MEAN_ROWS, 2 * HD), 0)
    for h, out in enumerate((a_ref, b_ref)):
        means = jnp.zeros((MEAN_ROWS, 2 * HD), jnp.float32)
        for i in range(PIECES // 2):
            s = h * (PIECES // 2) + i
            out[i * ROWS : (i + 1) * ROWS, :] = msg_ref[s, :ROWS, :]
            means = jnp.where(row == i, msg_ref[s, ROWS:, :].astype(jnp.float32), means)
        out[HALF:, :] = means.astype(jnp.bfloat16)


def unpack(msg):
    return pl.pallas_call(
        unpack_kernel,
        out_shape=[jax.ShapeDtypeStruct((HALF + MEAN_ROWS, 2 * HD), jnp.bfloat16)] * 2,
        compiler_params=params(16),
        cost_estimate=cost(1 << 18, MIB),
        name="unpack",
    )(msg)


def choose(refs, index, act):
    if len(refs) == 1:
        act(refs[0])
        return
    half = len(refs) // 2
    pl.when(index < half)(lambda: choose(refs[:half], index, act))
    pl.when(index >= half)(lambda: choose(refs[half:], index - half, act))


def pick_kernel(place_ref, picks_ref, *refs):
    bufs, below, above = refs[: 2 * NZ], refs[2 * NZ + 1], refs[2 * NZ + 2]
    out, low, high, sem, side_sem = refs[-5:]
    rows = WHALF // 2
    sides = [
        pltpu.make_async_copy(below.at[:rows, :], low, side_sem.at[0]),
        pltpu.make_async_copy(above.at[rows:, :], high, side_sem.at[1]),
    ]

    def step(n, carry):
        p = picks_ref[lax.div(n, PICKS), 1 + lax.rem(n, PICKS)]
        d = (place_ref[0] - lax.shift_right_logical(p, 3)) & (NZ - 1)
        h = lax.shift_right_logical(p, 2) & 1
        start = pl.multiple_of((p & 3) * ROWS, ROWS)
        to = pl.multiple_of(n * ROWS, ROWS)

        def act(buf):
            pltpu.make_async_copy(
                buf.at[pl.ds(start, ROWS), :], out.at[pl.ds(to, ROWS), :], sem
            ).start()

        choose(bufs, d * 2 + h, act)
        return carry

    for copy in sides:
        copy.start()
    lax.fori_loop(0, PIECES * PICKS, step, 0)
    pltpu.make_async_copy(out, out, sem).wait()
    for copy in sides:
        copy.wait()


def pick_pieces(place, picks, bufs, prev, below, above):
    half = jax.ShapeDtypeStruct((WHALF // 2, below.shape[1]), jnp.bfloat16)
    whole = lambda s: pl.BlockSpec(s.shape, lambda i, place, picks: (0, 0))
    pieces = jax.ShapeDtypeStruct((PIECES * PART, 2 * HD), jnp.bfloat16)
    side = jax.ShapeDtypeStruct(below.shape, below.dtype)
    return pl.pallas_call(
        pick_kernel,
        grid_spec=pltpu.PrefetchScalarGridSpec(
            num_scalar_prefetch=2,
            grid=(1,),
            in_specs=[ANY] * (2 * NZ + 3),
            out_specs=[ANY, ANY, whole(pieces), whole(half), whole(half)],
            scratch_shapes=[pltpu.SemaphoreType.DMA(()), pltpu.SemaphoreType.DMA((2,))],
        ),
        out_shape=[side, side, pieces, half, half],
        input_output_aliases={3 + 2 * NZ: 0, 4 + 2 * NZ: 1},
        compiler_params=params(60),
        cost_estimate=cost(0, MIB),
        name="pick_pieces",
    )(place, picks, *bufs, prev, below, above)


def contract(a, b):
    return lax.dot_general(a, b, (((1,), (1,)), ((), ())), preferred_element_type=jnp.float32)


def row_max(xs):
    top = jnp.max(xs[0], axis=1, keepdims=True)
    for x in xs[1:]:
        top = jnp.maximum(top, jnp.max(x, axis=1, keepdims=True))
    return top


def save_state(out_ref, rows, acc, top):
    lane = lax.broadcasted_iota(jnp.int32, (STACK, HD), 1)
    out_ref[rows, :HD] = acc[:, :HD]
    out_ref[rows, HD:] = jnp.where(lane < HD // 2, acc[:, HD:], top)


def near_kernel(place_ref, q_ref, k_ref, v_ref, prev_ref, stacked_ref, out_ref, own_v, prev_v):
    ones = jnp.ones((BLOCK, HD), jnp.bfloat16)
    own_v[:, :HD] = v_ref[...]
    own_v[:, HD:] = ones
    prev_v[:, :HD] = prev_ref[:, HD:]
    prev_v[:, HD:] = ones
    key = lax.broadcasted_iota(jnp.int32, (STACK, BLOCK), 1)
    token = lax.rem(lax.broadcasted_iota(jnp.int32, (STACK, BLOCK), 0), TILE)
    pen = jnp.where(place_ref[4] == 0, FAR, 0.0)

    def scores(i):
        at = pl.multiple_of(((place_ref[3] + i) & (NX - 1)) * TILE, TILE)
        for g in range(QPK):
            rows = slice(i * STACK + g * TILE, i * STACK + (g + 1) * TILE)
            stacked_ref[rows, :] = q_ref[pl.ds(at, TILE), g * HD : (g + 1) * HD]
        q = stacked_ref[i * STACK : (i + 1) * STACK, :]
        own = jnp.where(key - token <= at, contract(q, k_ref[...]) * SCALE, -FAR)
        return own, contract(q, prev_ref[:, :HD]) * SCALE

    after = scores(0)
    for i in range(NX):
        own, prev = after
        if i + 1 < NX:
            after = scores(i + 1)
        top = jnp.maximum(row_max([own]), row_max([prev]) - pen)
        own = jnp.exp2(own - top).astype(jnp.bfloat16)
        prev = jnp.exp2(prev - (top + pen)).astype(jnp.bfloat16)
        acc = jnp.dot(own, own_v[...], preferred_element_type=jnp.float32)
        acc += jnp.dot(prev, prev_v[...], preferred_element_type=jnp.float32)
        save_state(out_ref, slice(i * STACK, (i + 1) * STACK), acc, top)


def near_attention(place, q, k, v, prev):
    whole = lambda *shape: pl.BlockSpec(shape, lambda i, place: (0, 0))
    return pl.pallas_call(
        near_kernel,
        grid_spec=pltpu.PrefetchScalarGridSpec(
            num_scalar_prefetch=1,
            grid=(1,),
            in_specs=[
                whole(BLOCK, QPK * HD),
                whole(BLOCK, HD),
                whole(BLOCK, HD),
                whole(BLOCK, 2 * HD),
            ],
            out_specs=[whole(NX * STACK, HD), whole(NX * STACK, 2 * HD)],
            scratch_shapes=[pltpu.VMEM((BLOCK, 2 * HD), jnp.bfloat16)] * 2,
        ),
        out_shape=[
            jax.ShapeDtypeStruct((NX * STACK, HD), jnp.bfloat16),
            jax.ShapeDtypeStruct((NX * STACK, 2 * HD), jnp.float32),
        ],
        compiler_params=params(),
        cost_estimate=cost(1 << 20, MIB),
        name="near_attention",
    )(place, q, k, v, prev)


def summary_kernel(place_ref, q_ref, *refs):
    means, (out_ref, mean_k, mean_v) = refs[: 2 * NZ], refs[2 * NZ :]
    z, block = place_ref[0], place_ref[4]
    for s, mean in enumerate(means):
        rows = slice(s * MEAN_ROWS, (s + 1) * MEAN_ROWS)
        mean_k[rows, :] = mean[:, :HD]
        mean_v[rows, :HD] = mean[:, HD:]
    mean_v[:, HD:] = jnp.ones((2 * NZ * MEAN_ROWS, HD), jnp.bfloat16)

    s = lax.broadcasted_iota(jnp.int32, (1, 2 * NZ * MEAN_ROWS), 1)
    i4 = s & (MEAN_ROWS - 1)
    half = lax.shift_right_logical(s, 4) & 1
    zs = (z - lax.shift_right_logical(s, 5)) & (NZ - 1)
    number = zs * PIECES + half * (PIECES // 2) + i4
    bias = jnp.where((i4 < PIECES // 2) & (number < block), 0.0, -FAR)

    def scores(i):
        return contract(q_ref[i * STACK : (i + 1) * STACK, :], mean_k[...]) * SCALE + bias

    after = scores(0)
    for i in range(NX):
        sums = after
        if i + 1 < NX:
            after = scores(i + 1)
        top = jnp.maximum(row_max([sums]), 0.0)
        w = jnp.exp2(sums - top).astype(jnp.bfloat16)
        summary = jnp.dot(w, mean_v[...], preferred_element_type=jnp.float32)
        total = summary[:, HD:] + jnp.exp2(-top)
        out_ref[i * STACK : (i + 1) * STACK, :] = summary[:, :HD] / total


def summary_attention(place, q, bufs):
    whole = lambda rows, columns, at: pl.BlockSpec((rows, columns), lambda i, place: (at, 0))
    mean_count = 2 * NZ * MEAN_ROWS
    return pl.pallas_call(
        summary_kernel,
        grid_spec=pltpu.PrefetchScalarGridSpec(
            num_scalar_prefetch=1,
            grid=(1,),
            in_specs=[whole(NX * STACK, HD, 0)]
            + [whole(MEAN_ROWS, 2 * HD, HALF // MEAN_ROWS)] * (2 * NZ),
            out_specs=whole(NX * STACK, HD, 0),
            scratch_shapes=[
                pltpu.VMEM((mean_count, HD), jnp.bfloat16),
                pltpu.VMEM((mean_count, 2 * HD), jnp.bfloat16),
            ],
        ),
        out_shape=jax.ShapeDtypeStruct((NX * STACK, HD), jnp.float32),
        compiler_params=params(60),
        cost_estimate=cost(1 << 20, MIB),
        name="summary_attention",
    )(place, q, *bufs)


def far_values(place_ref, picks_ref, pieces_ref, v_all):
    block = place_ref[4]
    own = block & (PIECES - 1)
    for j in range(PICKS):
        p = picks_ref[own, j + 1]
        bad = p == block
        for e in range(j + 1):
            bad = bad | (p == picks_ref[own, e])
        keep = jnp.where(bad, 0.0, 1.0)
        ones = jnp.full((ROWS, HD), keep, jnp.float32).astype(jnp.bfloat16)
        for s in range(PIECES):
            at = slice(s * PART + j * ROWS, s * PART + (j + 1) * ROWS)
            v_all[at, :HD] = (pieces_ref[at, HD:].astype(jnp.float32) * keep).astype(jnp.bfloat16)
            v_all[at, HD:] = ones


def far_tiles(qs, states, pieces_ref, v_all, finish):
    chunks = [slice(n * BLOCK, (n + 1) * BLOCK) for n in range(PIECES * PART // BLOCK)]

    def scores(n):
        q = qs[n][...]
        return [contract(q, pieces_ref[chunk, :HD]) for chunk in chunks]

    after = scores(0)
    for n in range(len(qs)):
        xs = after
        if n + 1 < len(qs):
            after = scores(n + 1)
        state = states[n][...]
        top0 = state[:, 2 * HD - 1 :]
        top = jnp.maximum(top0, row_max(xs) * SCALE)
        acc = state * jnp.exp2(top0 - top)
        for chunk, x in zip(chunks, xs):
            w = jnp.exp2(x * SCALE - top).astype(jnp.bfloat16)
            acc += jnp.dot(w, v_all[chunk, :], preferred_element_type=jnp.float32)
        finish(n, acc, top)


def tile_spec(columns, at):
    return pl.BlockSpec((STACK, columns), lambda i, place, picks: (at, 0))


def whole_spec(rows, columns):
    return pl.BlockSpec((rows, columns), lambda i, place, picks: (0, 0))


def far_kernel(place_ref, picks_ref, q_ref, state_ref, summary_ref, pieces_ref, out_ref, v_all):
    tiles = [slice(n * STACK, (n + 1) * STACK) for n in range(NX)]

    def finish(n, acc, top):
        result = acc[:, :HD] / acc[:, HD : HD + 1] + summary_ref[tiles[n], :]
        result = result.astype(jnp.bfloat16)
        at = pl.multiple_of(((place_ref[3] + n) & (NX - 1)) * TILE, TILE)
        for g in range(QPK):
            out_ref[pl.ds(at, TILE), g * HD : (g + 1) * HD] = result[g * TILE : (g + 1) * TILE]

    @pl.when(place_ref[4] == 0)
    def _():
        for n in range(NX):
            finish(n, state_ref[tiles[n], :], None)

    @pl.when(place_ref[4] > 0)
    def _():
        far_values(place_ref, picks_ref, pieces_ref, v_all)
        far_tiles(
            [q_ref.at[t, :] for t in tiles],
            [state_ref.at[t, :] for t in tiles],
            pieces_ref,
            v_all,
            finish,
        )


def far_attention(place, picks, q, state, summary, pieces):
    whole = lambda *shape: pl.BlockSpec(shape, lambda i, place, picks: (0, 0))
    return pl.pallas_call(
        far_kernel,
        grid_spec=pltpu.PrefetchScalarGridSpec(
            num_scalar_prefetch=2,
            grid=(1,),
            in_specs=[
                whole(NX * STACK, HD),
                whole(NX * STACK, 2 * HD),
                whole(NX * STACK, HD),
                whole(PIECES * PART, 2 * HD),
            ],
            out_specs=whole(BLOCK, QPK * HD),
            scratch_shapes=[pltpu.VMEM((PIECES * PART, 2 * HD), jnp.bfloat16)],
        ),
        out_shape=jax.ShapeDtypeStruct((BLOCK, QPK * HD), jnp.bfloat16),
        compiler_params=params(),
        cost_estimate=cost(1 << 20, MIB),
        name="far_attention",
    )(place, picks, q, state, summary, pieces)


def hold_kernel(after_ref, low_ref, high_ref, low_out, high_out):
    pass


def hold(after, low, high):
    return pl.pallas_call(
        hold_kernel,
        in_specs=[ANY] * 3,
        out_specs=[ANY] * 2,
        out_shape=[jax.ShapeDtypeStruct(low.shape, low.dtype)] * 2,
        input_output_aliases={1: 0, 2: 1},
        compiler_params=params(16),
        cost_estimate=cost(0, 0),
        name="hold",
    )(after, low, high)


def project_kernel(place_ref, att_ref, w0, *refs):
    out_ref = refs[-1]
    x, c = place_ref[3], place_ref[2]
    depth = QPK * HD

    def columns(by, start, width):
        at = ((x + by) & (NX - 1)) * depth + start
        return att_ref[:, pl.ds(pl.multiple_of(at, width), width)]

    acc = jnp.dot(columns(0, 0, depth), w0[...], preferred_element_type=jnp.float32)
    for core, (below, above, low, high) in ((c, refs[:4]), (1 - c, refs[4:8])):
        opposite = jnp.concatenate([low[...], high[...]], axis=0)
        for by, w in ((-1, below[...]), (1, above[...]), (2, opposite)):
            a = columns(by, core * WHALF, WHALF)
            acc += jnp.dot(a, w, preferred_element_type=jnp.float32)
    out_ref[...] = acc.astype(jnp.bfloat16)


def project(place, attended, w0, weights):
    width, tile = w0.shape[1], 1024
    return pl.pallas_call(
        project_kernel,
        grid_spec=pltpu.PrefetchScalarGridSpec(
            num_scalar_prefetch=1,
            grid=(width // tile,),
            in_specs=[pl.BlockSpec((TILE, NX * QPK * HD), lambda n, place: (0, 0))]
            + [pl.BlockSpec((w.shape[0], tile), lambda n, place: (0, n)) for w in (w0, *weights)],
            out_specs=pl.BlockSpec((TILE, tile), lambda n, place: (0, n)),
        ),
        out_shape=jax.ShapeDtypeStruct((TILE, width), jnp.bfloat16),
        compiler_params=params(),
        cost_estimate=cost(1 << 20, MIB),
        name="project",
    )(place, attended, w0, *weights)


def shift(x, axis, size, by):
    return lax.ppermute(x, axis, [(i, (i + by) % size) for i in range(size)])


def swap(x):
    return lax.ppermute(x, "c", [(0, 1), (1, 0)])


def to_plane(x):
    return lax.all_to_all(x, ("y", "c"), 0, 0, tiled=True)


def per_device(q, k, v, picks, w):
    z, y, c, x = (lax.axis_index(a).astype(jnp.int32) for a in ("z", "y", "c", "x"))
    place = jnp.stack([z, y, c, x, z * PIECES + y * NC + c])
    plane_picks = lax.dynamic_slice_in_dim(picks.reshape(picks.shape[0], -1), z * PIECES, PIECES, 0)

    half = lax.dynamic_slice_in_dim(w, c * WHALF, WHALF, 0)
    sides = [shift(half, "x", NX, 1), shift(half, "x", NX, -1)]

    kv, msg = pack(k, v)
    a, b = unpack(to_plane(msg))
    blocks = NZ * PIECES
    prev = lax.ppermute(kv, ("z", "y", "c"), [(i, i + 1) for i in range(blocks - 1)])

    up, down = [(a, b)], [(a, b)]
    for d in range(3):
        up.append(tuple(shift(h, "z", NZ, 1) for h in up[-1]))
        down.append(tuple(shift(h, "z", NZ, -1) for h in down[-1]))
    far = (shift(up[3][0], "z", NZ, 1), shift(down[3][1], "z", NZ, -1))
    rings = up + [far] + [down[3], down[2], down[1]]
    bufs = [h for pair in rings for h in pair]

    below, above, pieces, low, high = pick_pieces(place, plane_picks, bufs, prev, *sides)
    pieces = to_plane(pieces)
    low, high = shift(low, "x", NX, 1), shift(high, "x", NX, -1)
    stacked, state = near_attention(place, q, k, v, prev)
    summary = summary_attention(place, stacked, bufs)
    attended = far_attention(place, plane_picks, stacked, state, summary, pieces)
    low, high = hold(attended, low, high)

    rows = lax.all_to_all(attended.reshape(NX, TILE, QPK * HD), "x", 0, 0, tiled=True)
    rows = jnp.transpose(rows, (1, 0, 2)).reshape(TILE, NX * QPK * HD)
    weights = [below, above, low, high]
    return project(place, rows, w, weights + [swap(m) for m in weights])


def solution(mesh):
    fine = Mesh(mesh.devices.reshape(NZ, NY, NC, NX), ("z", "y", "c", "x"))
    ctx = ("z", "y", "c")
    in_specs = (P(ctx, "x"), P(ctx, "x"), P(ctx, "x"), P(None, "x", None), P("x", None))
    out_specs = P(("z", "y", "c", "x"), None)
    return jax.shard_map(
        per_device, mesh=fine, in_specs=in_specs, out_specs=out_specs, check_vma=False
    )
```

profile of v0, /device:TPU:1, one launch (start us, length us, event | category | flops | bytes accessed | tf_op | source)
XLA Modules:
  0.0 129.1 jit_solution(2140574556164334550)
XLA Ops:
  0.0 3.2 %constant_dynamic-slice_fusion = bf16[256,4096]{1,0:T(8,128)(2,1)} fusion(bf16[512,4096]{1,0:T(8,128)(2,1)} %w0.1, s32[]{:T(128)S(6)} %select_n.7), kind=kLoop, calls=%fused_computation | loop fusion | bytes 4194308 | tf_op jit(solution)/shard_map/dynamic_slice | solution.py:449
  3.2 2.0 %collective-permute-start.15 = (bf16[256,4096]{1,0:T(8,128)(2,1)}, bf16[256,4096]{1,0:T(8,128)(2,1)S(1)}, u32[]{:S(2)}, u32[]{:S(2)}) collective-permute-start(bf16[256,4096]{1,0:T(8,128)(2,1)} %constant_dynamic-slice_fusion), channel_id=1, source_target_pairs={{0,1},{1,2},{2,3},{3,0},{4,5},{5,6},{6,7},{7,4},{8,9},{9,10},{10,1... | collective-permute-start | bytes 6291464 | tf_op jit(solution)/shard_map/ppermute | solution.py:433
  7.4 6.5 %all-to-all-start = ((bf16[8,80,256]{2,1,0:T(8,128)(2,1)}), bf16[8,80,256]{2,1,0:T(8,128)(2,1)S(1)}, u32[]{:S(2)}, u32[]{:S(2)}) async-start(bf16[8,80,256]{2,1,0:T(8,128)(2,1)} %get-tuple-element.21), calls=%async_computation | async-start | bytes 655360 | tf_op jit(solution)/shard_map/all_to_all | solution.py:441
  13.9 3.5 %collective-permute-start = (bf16[512,256]{1,0:T(8,128)(2,1)S(1)}, bf16[512,256]{1,0:T(8,128)(2,1)S(1)}, u32[]{:S(2)}, u32[]{:S(2)}) collective-permute-start(bf16[512,256]{1,0:T(8,128)(2,1)S(1)} %get-tuple-element.18), channel_id=1, source_target_pairs={{0,4},{4,8},{8,12},{12,16},{16,20},{20,24},{24,28},{28,32},{32,36}... | collective-permute-start | bytes 786440 | tf_op jit(solution)/shard_map/ppermute | solution.py:455
  17.4 3.6 %all-to-all-done.msg_ref = bf16[8,80,256]{2,1,0:T(8,128)(2,1)S(1)} async-done(((bf16[8,80,256]{2,1,0:T(8,128)(2,1)}), bf16[8,80,256]{2,1,0:T(8,128)(2,1)S(1)}, u32[]{:S(2)}, u32[]{:S(2)}) %all-to-all-start) | async-done | bytes 327712 | tf_op jit(solution)/shard_map/all_to_all | solution.py:441
  21.1 5.9 %collective-permute-start.8 = (bf16[272,256]{1,0:T(8,128)(2,1)S(1)}, bf16[272,256]{1,0:T(8,128)(2,1)S(1)}, u32[]{:S(2)}, u32[]{:S(2)}) collective-permute-start(bf16[272,256]{1,0:T(8,128)(2,1)S(1)} %get-tuple-element.23.refs_1_), channel_id=1, source_target_pairs={{0,224},{32,0},{64,32},{96,64},{128,96},{160,128},{192,160},{224,1... | collective-permute-start | bytes 417800 | tf_op jit(solution)/shard_map/ppermute | solution.py:433
  27.0 2.7 %collective-permute-start.12 = (bf16[272,256]{1,0:T(8,128)(2,1)S(1)}, bf16[272,256]{1,0:T(8,128)(2,1)S(1)}, u32[]{:S(2)}, u32[]{:S(2)}) collective-permute-start(bf16[272,256]{1,0:T(8,128)(2,1)S(1)} %get-tuple-element.22.refs_0_), channel_id=1, source_target_pairs={{0,224},{32,0},{64,32},{96,64},{128,96},{160,128},{192,160},{224,1... | collective-permute-start | bytes 417800 | tf_op jit(solution)/shard_map/ppermute | solution.py:433
  29.7 2.7 %collective-permute-done.1.refs_2_ = bf16[272,256]{1,0:T(8,128)(2,1)S(1)} collective-permute-done((bf16[272,256]{1,0:T(8,128)(2,1)S(1)}, bf16[272,256]{1,0:T(8,128)(2,1)S(1)}, u32[]{:S(2)}, u32[]{:S(2)}) %collective-permute-start.1) | collective-permute-done | bytes 139296 | tf_op jit(solution)/shard_map/ppermute | solution.py:433
  33.9 2.4 %collective-permute-done.2.refs_3_ = bf16[272,256]{1,0:T(8,128)(2,1)S(1)} collective-permute-done((bf16[272,256]{1,0:T(8,128)(2,1)S(1)}, bf16[272,256]{1,0:T(8,128)(2,1)S(1)}, u32[]{:S(2)}, u32[]{:S(2)}) %collective-permute-start.2) | collective-permute-done | bytes 139296 | tf_op jit(solution)/shard_map/ppermute | solution.py:433
  37.7 2.4 %collective-permute-done.3.refs_4_ = bf16[272,256]{1,0:T(8,128)(2,1)S(1)} collective-permute-done((bf16[272,256]{1,0:T(8,128)(2,1)S(1)}, bf16[272,256]{1,0:T(8,128)(2,1)S(1)}, u32[]{:S(2)}, u32[]{:S(2)}) %collective-permute-start.3) | collective-permute-done | bytes 139296 | tf_op jit(solution)/shard_map/ppermute | solution.py:433
  41.6 1.7 %collective-permute-done.4.refs_5_ = bf16[272,256]{1,0:T(8,128)(2,1)} collective-permute-done((bf16[272,256]{1,0:T(8,128)(2,1)S(1)}, bf16[272,256]{1,0:T(8,128)(2,1)}, u32[]{:S(2)}, u32[]{:S(2)}) %collective-permute-start.4) | collective-permute-done | bytes 139296 | tf_op jit(solution)/shard_map/ppermute | solution.py:433
  45.1 2.1 %collective-permute-done.5.refs_6_ = bf16[272,256]{1,0:T(8,128)(2,1)} collective-permute-done((bf16[272,256]{1,0:T(8,128)(2,1)S(1)}, bf16[272,256]{1,0:T(8,128)(2,1)}, u32[]{:S(2)}, u32[]{:S(2)}) %collective-permute-start.5) | collective-permute-done | bytes 139296 | tf_op jit(solution)/shard_map/ppermute | solution.py:433
  47.2 1.4 %collective-permute-start.11 = (bf16[272,256]{1,0:T(8,128)(2,1)}, bf16[272,256]{1,0:T(8,128)(2,1)}, u32[]{:S(2)}, u32[]{:S(2)}) collective-permute-start(bf16[272,256]{1,0:T(8,128)(2,1)} %collective-permute-done.10.refs_11_), channel_id=1, source_target_pairs={{0,224},{32,0},{64,32},{96,64},{128,96},{160,128},{192,160},{224,1... | collective-permute-start | bytes 417800 | tf_op jit(solution)/shard_map/ppermute | solution.py:433
  51.7 3.6 %collective-permute-done.7.refs_8_ = bf16[272,256]{1,0:T(8,128)(2,1)} collective-permute-done((bf16[272,256]{1,0:T(8,128)(2,1)}, bf16[272,256]{1,0:T(8,128)(2,1)}, u32[]{:S(2)}, u32[]{:S(2)}) %collective-permute-start.7) | collective-permute-done | bytes 139296 | tf_op jit(solution)/shard_map/ppermute | solution.py:433
  56.6 6.6 %pick_pieces.1 = (bf16[256,4096]{1,0:T(8,128)(2,1)}, bf16[256,4096]{1,0:T(8,128)(2,1)}, bf16[3072,256]{1,0:T(8,128)(2,1)}, bf16[128,4096]{1,0:T(8,128)(2,1)}, bf16[128,4096]{1,0:T(8,128)(2,1)}) custom-call(s32[5]{0:T(128)} %stack.23.place_ref, s32[8,7]{1,0:T(8,128)} %bitcast.14, ...), custom_call_target="tpu_custom_call", output_to_operand_aliasing={{0}: (19, {}), {1}: (20, {})} | custom-call | bytes 1048576 | tf_op jit(solution)/shard_map/pick_pieces/pallas_call | solution.py:137
  63.3 10.5 %all-to-all-start.1 = ((bf16[8,384,256]{2,1,0:T(8,128)(2,1)}), bf16[8,384,256]{2,1,0:T(8,128)(2,1)}, u32[]{:S(2)}, u32[]{:S(2)}) async-start(bf16[8,384,256]{2,1,0:T(8,128)(2,1)} %bitcast.17), calls=%async_computation.1 | async-start | bytes 3145728 | tf_op jit(solution)/shard_map/all_to_all | solution.py:441
  73.8 2.7 %collective-permute-start.18 = (bf16[128,4096]{1,0:T(8,128)(2,1)}, bf16[128,4096]{1,0:T(8,128)(2,1)}, u32[]{:S(2)}, u32[]{:S(2)}) collective-permute-start(bf16[128,4096]{1,0:T(8,128)(2,1)} %get-tuple-element.28), channel_id=1, source_target_pairs={{0,3},{1,0},{2,1},{3,2},{4,7},{5,4},{6,5},{7,6},{8,11},{9,8},{10,9... | collective-permute-start | bytes 3145736 | tf_op jit(solution)/shard_map/ppermute | solution.py:433
  79.2 3.6 %near_attention.1 = (bf16[2048,128]{1,0:T(8,128)(2,1)S(1)}, f32[2048,256]{1,0:T(8,128)S(1)}) custom-call(s32[5]{0:T(128)S(1)} %copy-done.18, bf16[512,512]{1,0:T(8,128)(2,1)S(1)} %copy-done.12, bf16[512,128]{1,0:T(8,128)(2,1)S(1)} %copy-done.14, bf16[512,128]{1,0:T(8,128)(2,1)S(1)} %copy-done.16, bf16[512,256]{1,0:T(8,128)(2,1)S(1)} %copy-done.9), custom_call_target="tpu_custom_call" | custom-call | flops 1048576 | bytes 1048576 | tf_op jit(solution)/shard_map/near_attention/pallas_call | solution.py:205
  85.0 3.9 %summary_attention.1.summary_ref = f32[2048,128]{1,0:T(8,128)} custom-call(s32[5]{0:T(128)} %stack.23.place_ref, bf16[2048,128]{1,0:T(8,128)(2,1)} %copy-done.6, bf16[272,256]{1,0:T(8,128)(2,1)} %copy-done.10, bf16[272,256]{1,0:T(8,128)(2,1)} %copy-done.11, bf16[272,256]{1,0:T(8,128)(2,1)} %copy-done.21, bf16[272,256]{1,0:T(8,128)(2,1)} %copy-done.23, ...), custom_call_target="tpu_custom_call" | custom-call | flops 1048576 | bytes 1048576 | tf_op jit(solution)/shard_map/summary_attention/pallas_call | solution.py:263
  88.9 5.7 %all-to-all-done.1 = bf16[8,384,256]{2,1,0:T(8,128)(2,1)} async-done(((bf16[8,384,256]{2,1,0:T(8,128)(2,1)}), bf16[8,384,256]{2,1,0:T(8,128)(2,1)}, u32[]{:S(2)}, u32[]{:S(2)}) %all-to-all-start.1) | async-done | bytes 1572896 | tf_op jit(solution)/shard_map/all_to_all | solution.py:441
  95.8 1.6 %copy-done.5 = f32[2048,256]{1,0:T(8,128)S(1)} copy-done((f32[2048,256]{1,0:T(8,128)S(1)}, f32[2048,256]{1,0:T(8,128)}, u32[]{:S(2)}) %copy-start.5) | copy-done | bytes 2097176
  98.5 10.5 %far_attention.1.after_ref = bf16[512,512]{1,0:T(8,128)(2,1)S(1)} custom-call(s32[5]{0:T(128)S(1)} %copy-done.19, s32[8,7]{1,0:T(8,128)S(1)} %bitcast.15, bf16[2048,128]{1,0:T(8,128)(2,1)S(1)} %copy-done.7, f32[2048,256]{1,0:T(8,128)S(1)} %copy-done.5, f32[2048,128]{1,0:T(8,128)S(1)} %copy-done.3, bf16[3072,256]{1,0:T(8,128)(2,1)} %bitcast.7.pieces_ref), custom_call_target="tpu_custom_call" | custom-call | flops 1048576 | bytes 1048576 | tf_op jit(solution)/shard_map/far_attention/pallas_call | solution.py:358
  109.6 11.8 %all_to_all.21 = bf16[4,128,512]{2,1,0:T(8,128)(2,1)S(1)} all-to-all(bf16[4,128,512]{2,1,0:T(8,128)(2,1)S(1)} %bitcast.12), channel_id=1, replica_groups=mesh['z'=8,'y'=4,'c'=2,'x'=4] {'x'}, dimensions={0} | all-to-all | bytes 1048576 | tf_op jit(solution)/shard_map/all_to_all | solution.py:473
  121.5 7.5 %project.1 = bf16[128,4096]{1,0:T(8,128)(2,1)} custom-call(s32[5]{0:T(128)S(1)} %copy-done.19, bf16[128,2048]{1,0:T(8,128)(2,1)S(1)} %bitcast.13, bf16[512,4096]{1,0:T(8,128)(2,1)} %w0.1, bf16[256,4096]{1,0:T(8,128)(2,1)S(1)} %copy-done.2, bf16[256,4096]{1,0:T(8,128)(2,1)} %get-tuple-element.26.refs_1_, bf16[128,4096]{1,0:T(8,128)(2,1)S(1)} %get-tuple-element.29.refs_2_, ...), custom_call_target="tpu_custom_call" | custom-call | flops 1048576 | bytes 1048576 | tf_op jit(solution)/shard_map/project/pallas_call | solution.py:416
  (96 shorter events, 20.5 us)
Async XLA Ops:
  3.2 52.0 %collective-permute-start.15 = (bf16[256,4096]{1,0:T(8,128)(2,1)}, bf16[256,4096]{1,0:T(8,128)(2,1)S(1)}, u32[]{:S(2)}, u32[]{:S(2)}) collective-permute-start(bf16[256,4096]{1,0:T(8,128)(2,1)} %constant_dynamic-slice_fusion), channel_id=1, source_target_pairs={{0,1},{1,2},{2,3},{3,0},{4,5},{5,6},{6,7},{7,4},{8,9},{9,10},{10,1... | collective-permute-start | bytes 6291464 | tf_op jit(solution)/shard_map/ppermute | solution.py:433
  5.3 50.0 %collective-permute-start.16 = (bf16[256,4096]{1,0:T(8,128)(2,1)}, bf16[256,4096]{1,0:T(8,128)(2,1)}, u32[]{:S(2)}, u32[]{:S(2)}) collective-permute-start(bf16[256,4096]{1,0:T(8,128)(2,1)} %constant_dynamic-slice_fusion), channel_id=1, source_target_pairs={{0,3},{1,0},{2,1},{3,2},{4,7},{5,4},{6,5},{7,6},{8,11},{9,8},{10,9... | collective-permute-start | bytes 6291464 | tf_op jit(solution)/shard_map/ppermute | solution.py:433
  7.4 13.7 %all-to-all-start = ((bf16[8,80,256]{2,1,0:T(8,128)(2,1)}), bf16[8,80,256]{2,1,0:T(8,128)(2,1)S(1)}, u32[]{:S(2)}, u32[]{:S(2)}) async-start(bf16[8,80,256]{2,1,0:T(8,128)(2,1)} %get-tuple-element.21), calls=%async_computation | async-start | bytes 655360 | tf_op jit(solution)/shard_map/all_to_all | solution.py:441
  13.9 13.1 %collective-permute-start = (bf16[512,256]{1,0:T(8,128)(2,1)S(1)}, bf16[512,256]{1,0:T(8,128)(2,1)S(1)}, u32[]{:S(2)}, u32[]{:S(2)}) collective-permute-start(bf16[512,256]{1,0:T(8,128)(2,1)S(1)} %get-tuple-element.18), channel_id=1, source_target_pairs={{0,4},{4,8},{8,12},{12,16},{16,20},{20,24},{24,28},{28,32},{32,36}... | collective-permute-start | bytes 786440 | tf_op jit(solution)/shard_map/ppermute | solution.py:455
  21.1 8.5 %collective-permute-start.8 = (bf16[272,256]{1,0:T(8,128)(2,1)S(1)}, bf16[272,256]{1,0:T(8,128)(2,1)S(1)}, u32[]{:S(2)}, u32[]{:S(2)}) collective-permute-start(bf16[272,256]{1,0:T(8,128)(2,1)S(1)} %get-tuple-element.23.refs_1_), channel_id=1, source_target_pairs={{0,224},{32,0},{64,32},{96,64},{128,96},{160,128},{192,160},{224,1... | collective-permute-start | bytes 417800 | tf_op jit(solution)/shard_map/ppermute | solution.py:433
  27.0 5.4 %collective-permute-start.1 = (bf16[272,256]{1,0:T(8,128)(2,1)S(1)}, bf16[272,256]{1,0:T(8,128)(2,1)S(1)}, u32[]{:S(2)}, u32[]{:S(2)}) collective-permute-start(bf16[272,256]{1,0:T(8,128)(2,1)S(1)} %get-tuple-element.22.refs_0_), channel_id=1, source_target_pairs={{0,32},{32,64},{64,96},{96,128},{128,160},{160,192},{192,224},{224... | collective-permute-start | bytes 417800 | tf_op jit(solution)/shard_map/ppermute | solution.py:433
  27.0 5.6 %collective-permute-start.12 = (bf16[272,256]{1,0:T(8,128)(2,1)S(1)}, bf16[272,256]{1,0:T(8,128)(2,1)S(1)}, u32[]{:S(2)}, u32[]{:S(2)}) collective-permute-start(bf16[272,256]{1,0:T(8,128)(2,1)S(1)} %get-tuple-element.22.refs_0_), channel_id=1, source_target_pairs={{0,224},{32,0},{64,32},{96,64},{128,96},{160,128},{192,160},{224,1... | collective-permute-start | bytes 417800 | tf_op jit(solution)/shard_map/ppermute | solution.py:433
  29.7 6.6 %collective-permute-start.2 = (bf16[272,256]{1,0:T(8,128)(2,1)S(1)}, bf16[272,256]{1,0:T(8,128)(2,1)S(1)}, u32[]{:S(2)}, u32[]{:S(2)}) collective-permute-start(bf16[272,256]{1,0:T(8,128)(2,1)S(1)} %get-tuple-element.23.refs_1_), channel_id=1, source_target_pairs={{0,32},{32,64},{64,96},{96,128},{128,160},{160,192},{192,224},{224... | collective-permute-start | bytes 417800 | tf_op jit(solution)/shard_map/ppermute | solution.py:433
  32.6 7.6 %collective-permute-start.3 = (bf16[272,256]{1,0:T(8,128)(2,1)S(1)}, bf16[272,256]{1,0:T(8,128)(2,1)S(1)}, u32[]{:S(2)}, u32[]{:S(2)}) collective-permute-start(bf16[272,256]{1,0:T(8,128)(2,1)S(1)} %collective-permute-done.1.refs_2_), channel_id=1, source_target_pairs={{0,32},{32,64},{64,96},{96,128},{128,160},{160,192},{192,224},{224... | collective-permute-start | bytes 417800 | tf_op jit(solution)/shard_map/ppermute | solution.py:433
  36.3 5.2 %collective-permute-start.13 = (bf16[272,256]{1,0:T(8,128)(2,1)S(1)}, bf16[272,256]{1,0:T(8,128)(2,1)S(1)}, u32[]{:S(2)}, u32[]{:S(2)}) collective-permute-start(bf16[272,256]{1,0:T(8,128)(2,1)S(1)} %collective-permute-done.12.refs_14_), channel_id=1, source_target_pairs={{0,224},{32,0},{64,32},{96,64},{128,96},{160,128},{192,160},{224,1... | collective-permute-start | bytes 417800 | tf_op jit(solution)/shard_map/ppermute | solution.py:433
  36.7 6.6 %collective-permute-start.4 = (bf16[272,256]{1,0:T(8,128)(2,1)S(1)}, bf16[272,256]{1,0:T(8,128)(2,1)}, u32[]{:S(2)}, u32[]{:S(2)}) collective-permute-start(bf16[272,256]{1,0:T(8,128)(2,1)S(1)} %collective-permute-done.2.refs_3_), channel_id=1, source_target_pairs={{0,32},{32,64},{64,96},{96,128},{128,160},{160,192},{192,224},{224... | collective-permute-start | bytes 417800 | tf_op jit(solution)/shard_map/ppermute | solution.py:433
  40.2 4.9 %collective-permute-start.10 = (bf16[272,256]{1,0:T(8,128)(2,1)S(1)}, bf16[272,256]{1,0:T(8,128)(2,1)}, u32[]{:S(2)}, u32[]{:S(2)}) collective-permute-start(bf16[272,256]{1,0:T(8,128)(2,1)S(1)} %collective-permute-done.9.refs_13_), channel_id=1, source_target_pairs={{0,224},{32,0},{64,32},{96,64},{128,96},{160,128},{192,160},{224,1... | collective-permute-start | bytes 417800 | tf_op jit(solution)/shard_map/ppermute | solution.py:433
  41.5 5.6 %collective-permute-start.5 = (bf16[272,256]{1,0:T(8,128)(2,1)S(1)}, bf16[272,256]{1,0:T(8,128)(2,1)}, u32[]{:S(2)}, u32[]{:S(2)}) collective-permute-start(bf16[272,256]{1,0:T(8,128)(2,1)S(1)} %collective-permute-done.3.refs_4_), channel_id=1, source_target_pairs={{0,32},{32,64},{64,96},{96,128},{128,160},{160,192},{192,224},{224... | collective-permute-start | bytes 417800 | tf_op jit(solution)/shard_map/ppermute | solution.py:433
  43.3 5.3 %collective-permute-start.14 = (bf16[272,256]{1,0:T(8,128)(2,1)S(1)}, bf16[272,256]{1,0:T(8,128)(2,1)S(1)}, u32[]{:S(2)}, u32[]{:S(2)}) collective-permute-start(bf16[272,256]{1,0:T(8,128)(2,1)S(1)} %collective-permute-done.13.refs_12_), channel_id=1, source_target_pairs={{0,224},{32,0},{64,32},{96,64},{128,96},{160,128},{192,160},{224,1... | collective-permute-start | bytes 417800 | tf_op jit(solution)/shard_map/ppermute | solution.py:433
  45.1 5.6 %collective-permute-start.6 = (bf16[272,256]{1,0:T(8,128)(2,1)}, bf16[272,256]{1,0:T(8,128)(2,1)}, u32[]{:S(2)}, u32[]{:S(2)}) collective-permute-start(bf16[272,256]{1,0:T(8,128)(2,1)} %collective-permute-done.4.refs_5_), channel_id=1, source_target_pairs={{0,32},{32,64},{64,96},{96,128},{128,160},{160,192},{192,224},{224... | collective-permute-start | bytes 417800 | tf_op jit(solution)/shard_map/ppermute | solution.py:433
  47.2 4.5 %collective-permute-start.11 = (bf16[272,256]{1,0:T(8,128)(2,1)}, bf16[272,256]{1,0:T(8,128)(2,1)}, u32[]{:S(2)}, u32[]{:S(2)}) collective-permute-start(bf16[272,256]{1,0:T(8,128)(2,1)} %collective-permute-done.10.refs_11_), channel_id=1, source_target_pairs={{0,224},{32,0},{64,32},{96,64},{128,96},{160,128},{192,160},{224,1... | collective-permute-start | bytes 417800 | tf_op jit(solution)/shard_map/ppermute | solution.py:433
  49.2 6.0 %collective-permute-start.7 = (bf16[272,256]{1,0:T(8,128)(2,1)}, bf16[272,256]{1,0:T(8,128)(2,1)}, u32[]{:S(2)}, u32[]{:S(2)}) collective-permute-start(bf16[272,256]{1,0:T(8,128)(2,1)} %collective-permute-done.5.refs_6_), channel_id=1, source_target_pairs={{0,32},{32,64},{64,96},{96,128},{128,160},{160,192},{192,224},{224... | collective-permute-start | bytes 417800 | tf_op jit(solution)/shard_map/ppermute | solution.py:433
  63.3 31.3 %all-to-all-start.1 = ((bf16[8,384,256]{2,1,0:T(8,128)(2,1)}), bf16[8,384,256]{2,1,0:T(8,128)(2,1)}, u32[]{:S(2)}, u32[]{:S(2)}) async-start(bf16[8,384,256]{2,1,0:T(8,128)(2,1)} %bitcast.17), calls=%async_computation.1 | async-start | bytes 3145728 | tf_op jit(solution)/shard_map/all_to_all | solution.py:441
  73.8 35.2 %collective-permute-start.17 = (bf16[128,4096]{1,0:T(8,128)(2,1)}, bf16[128,4096]{1,0:T(8,128)(2,1)S(1)}, u32[]{:S(2)}, u32[]{:S(2)}) collective-permute-start(bf16[128,4096]{1,0:T(8,128)(2,1)} %get-tuple-element.27), channel_id=1, source_target_pairs={{0,1},{1,2},{2,3},{3,0},{4,5},{5,6},{6,7},{7,4},{8,9},{9,10},{10,1... | collective-permute-start | bytes 3145736 | tf_op jit(solution)/shard_map/ppermute | solution.py:433
  73.8 35.3 %collective-permute-start.18 = (bf16[128,4096]{1,0:T(8,128)(2,1)}, bf16[128,4096]{1,0:T(8,128)(2,1)}, u32[]{:S(2)}, u32[]{:S(2)}) collective-permute-start(bf16[128,4096]{1,0:T(8,128)(2,1)} %get-tuple-element.28), channel_id=1, source_target_pairs={{0,3},{1,0},{2,1},{3,2},{4,7},{5,4},{6,5},{7,6},{8,11},{9,8},{10,9... | collective-permute-start | bytes 3145736 | tf_op jit(solution)/shard_map/ppermute | solution.py:433
  76.4 45.0 %collective-permute-start.19 = (bf16[256,4096]{1,0:T(8,128)(2,1)S(1)}, bf16[256,4096]{1,0:T(8,128)(2,1)}, u32[]{:S(2)}, u32[]{:S(2)}) collective-permute-start(bf16[256,4096]{1,0:T(8,128)(2,1)S(1)} %copy-done.2), channel_id=1, source_target_pairs={{0,4},{4,0},{1,5},{5,1},{2,6},{6,2},{3,7},{7,3},{8,12},{12,8},{9,1... | collective-permute-start | bytes 6291464 | tf_op jit(solution)/shard_map/ppermute | solution.py:437
  77.2 44.3 %collective-permute-start.20 = (bf16[256,4096]{1,0:T(8,128)(2,1)}, bf16[256,4096]{1,0:T(8,128)(2,1)}, u32[]{:S(2)}, u32[]{:S(2)}) collective-permute-start(bf16[256,4096]{1,0:T(8,128)(2,1)} %get-tuple-element.26.refs_1_), channel_id=1, source_target_pairs={{0,4},{4,0},{1,5},{5,1},{2,6},{6,2},{3,7},{7,3},{8,12},{12,8},{9,1... | collective-permute-start | bytes 6291464 | tf_op jit(solution)/shard_map/ppermute | solution.py:437
  109.0 12.5 %collective-permute-start.21 = (bf16[128,4096]{1,0:T(8,128)(2,1)S(1)}, bf16[128,4096]{1,0:T(8,128)(2,1)S(1)}, u32[]{:S(2)}, u32[]{:S(2)}) collective-permute-start(bf16[128,4096]{1,0:T(8,128)(2,1)S(1)} %get-tuple-element.29.refs_2_), channel_id=1, source_target_pairs={{0,4},{4,0},{1,5},{5,1},{2,6},{6,2},{3,7},{7,3},{8,12},{12,8},{9,1... | collective-permute-start | bytes 3145736 | tf_op jit(solution)/shard_map/ppermute | solution.py:437
  109.1 12.4 %collective-permute-start.22 = (bf16[128,4096]{1,0:T(8,128)(2,1)}, bf16[128,4096]{1,0:T(8,128)(2,1)S(1)}, u32[]{:S(2)}, u32[]{:S(2)}) collective-permute-start(bf16[128,4096]{1,0:T(8,128)(2,1)} %get-tuple-element.30.refs_3_), channel_id=1, source_target_pairs={{0,4},{4,0},{1,5},{5,1},{2,6},{6,2},{3,7},{7,3},{8,12},{12,8},{9,1... | collective-permute-start | bytes 3145736 | tf_op jit(solution)/shard_map/ppermute | solution.py:437
  (29 other events, 367.2 us)
where the time goes:
time: 130 us; the launch traced here: 129 us
  starting transfers between devices  43.2 us (33%)
  Pallas kernels  33.1 us (25%)
  waiting for transfers between devices  26.1 us (20%)
  local copies, waits for them, and re-layouts  14.6 us (11%)
  blocking collectives  11.8 us (9%)
    ppermute x18, starting transfers between devices, shift(): return lax.ppermute(x, axis, [(i, (i + by) % size) for i in range(size)])  21.3 us
    all_to_all x2, starting transfers between devices, to_plane(): return lax.all_to_all(x, ('y', 'c'), 0, 0, tiled=True)  17 us
    ppermute x18, waiting for transfers between devices, shift(): return lax.ppermute(x, axis, [(i, (i + by) % size) for i in range(size)])  16.8 us
    all_to_all x1, blocking collectives, per_device(): lax.all_to_all(attended.reshape(NX, TILE, QPK * HD), 'x', 0, 0, tiled=True)  11.8 us
    unnamed x57, local copies, waits for them, and re-layouts  10.6 us
    pallas_call x1, Pallas kernels, far_attention(): pl.pallas_call(far_kernel, grid_spec=pltpu.PrefetchScalarGridSpec(num_sca...  10.5 us
    all_to_all x2, waiting for transfers between devices, to_plane(): return lax.all_to_all(x, ('y', 'c'), 0, 0, tiled=True)  9.3 us
    pallas_call x1, Pallas kernels, project(): pl.pallas_call(project_kernel, grid_spec=pltpu.PrefetchScalarGridSpec(num...  7.53 us
  transfers between devices with their start and end apart: 25, of which 13 were waited for; matrix products, arithmetic and copies ran while one was open for 1% of the time, Pallas kernels for 15%

commit v1 on v0

--- a/solution.py
+++ b/solution.py
@@ -296,40 +296,40 @@
             v_all[at, HD:] = ones
 
 
-def far_tiles(qs, states, pieces_ref, v_all, finish):
-    chunks = [slice(n * BLOCK, (n + 1) * BLOCK) for n in range(PIECES * PART // BLOCK)]
-
-    def scores(n):
-        q = qs[n][...]
-        return [contract(q, pieces_ref[chunk, :HD]) for chunk in chunks]
-
-    after = scores(0)
-    for n in range(len(qs)):
-        xs = after
-        if n + 1 < len(qs):
-            after = scores(n + 1)
-        state = states[n][...]
-        top0 = state[:, 2 * HD - 1 :]
-        top = jnp.maximum(top0, row_max(xs) * SCALE)
-        acc = state * jnp.exp2(top0 - top)
-        for chunk, x in zip(chunks, xs):
-            w = jnp.exp2(x * SCALE - top).astype(jnp.bfloat16)
-            acc += jnp.dot(w, v_all[chunk, :], preferred_element_type=jnp.float32)
-        finish(n, acc, top)
-
-
-def tile_spec(columns, at):
-    return pl.BlockSpec((STACK, columns), lambda i, place, picks: (at, 0))
-
-
-def whole_spec(rows, columns):
-    return pl.BlockSpec((rows, columns), lambda i, place, picks: (0, 0))
-
-
-def far_kernel(place_ref, picks_ref, q_ref, state_ref, summary_ref, pieces_ref, out_ref, v_all):
-    tiles = [slice(n * STACK, (n + 1) * STACK) for n in range(NX)]
-
-    def finish(n, acc, top):
+def far_kernel(
+    place_ref,
+    picks_ref,
+    q_ref,
+    pieces_ref,
+    state_hbm,
+    summary_hbm,
+    out_ref,
+    v_all,
+    state_ref,
+    summary_ref,
+    sems,
+):
+    tiles = [pl.ds(n * STACK, STACK) for n in range(NX)]
+    copies = []
+    for n, tile in enumerate(tiles):
+        copies.append(
+            (
+                pltpu.make_async_copy(state_hbm.at[tile, :], state_ref.at[tile, :], sems.at[0, n]),
+                pltpu.make_async_copy(
+                    summary_hbm.at[tile, :], summary_ref.at[tile, :], sems.at[1, n]
+                ),
+            )
+        )
+    for pair in copies:
+        for copy in pair:
+            copy.start()
+
+    def arrive():
+        for pair in copies:
+            for copy in pair:
+                copy.wait()
+
+    def finish(n, acc):
         result = acc[:, :HD] / acc[:, HD : HD + 1] + summary_ref[tiles[n], :]
         result = result.astype(jnp.bfloat16)
         at = pl.multiple_of(((place_ref[3] + n) & (NX - 1)) * TILE, TILE)
@@ -338,19 +338,33 @@
 
     @pl.when(place_ref[4] == 0)
     def _():
+        arrive()
         for n in range(NX):
-            finish(n, state_ref[tiles[n], :], None)
+            finish(n, state_ref[tiles[n], :])
 
     @pl.when(place_ref[4] > 0)
     def _():
+        chunks = [slice(n * BLOCK, (n + 1) * BLOCK) for n in range(PIECES * PART // BLOCK)]
+
+        def scores(n):
+            q = q_ref[tiles[n], :]
+            return [contract(q, pieces_ref[chunk, :HD]) for chunk in chunks]
+
         far_values(place_ref, picks_ref, pieces_ref, v_all)
-        far_tiles(
-            [q_ref.at[t, :] for t in tiles],
-            [state_ref.at[t, :] for t in tiles],
-            pieces_ref,
-            v_all,
-            finish,
-        )
+        arrive()
+        after = scores(0)
+        for n in range(NX):
+            xs = after
+            if n + 1 < NX:
+                after = scores(n + 1)
+            state = state_ref[tiles[n], :]
+            top0 = state[:, 2 * HD - 1 :]
+            top = jnp.maximum(top0, row_max(xs) * SCALE)
+            acc = state * jnp.exp2(top0 - top)
+            for chunk, x in zip(chunks, xs):
+                w = jnp.exp2(x * SCALE - top).astype(jnp.bfloat16)
+                acc += jnp.dot(w, v_all[chunk, :], preferred_element_type=jnp.float32)
+            finish(n, acc)
 
 
 def far_attention(place, picks, q, state, summary, pieces):
@@ -360,20 +374,20 @@
         grid_spec=pltpu.PrefetchScalarGridSpec(
             num_scalar_prefetch=2,
             grid=(1,),
-            in_specs=[
-                whole(NX * STACK, HD),
-                whole(NX * STACK, 2 * HD),
-                whole(NX * STACK, HD),
-                whole(PIECES * PART, 2 * HD),
+            in_specs=[whole(NX * STACK, HD), whole(PIECES * PART, 2 * HD), ANY, ANY],
+            out_specs=whole(BLOCK, QPK * HD),
+            scratch_shapes=[
+                pltpu.VMEM((PIECES * PART, 2 * HD), jnp.bfloat16),
+                pltpu.VMEM((NX * STACK, 2 * HD), jnp.float32),
+                pltpu.VMEM((NX * STACK, HD), jnp.float32),
+                pltpu.SemaphoreType.DMA((2, NX)),
             ],
-            out_specs=whole(BLOCK, QPK * HD),
-            scratch_shapes=[pltpu.VMEM((PIECES * PART, 2 * HD), jnp.bfloat16)],
         ),
         out_shape=jax.ShapeDtypeStruct((BLOCK, QPK * HD), jnp.bfloat16),
-        compiler_params=params(),
+        compiler_params=params(60),
         cost_estimate=cost(1 << 20, MIB),
         name="far_attention",
-    )(place, picks, q, state, summary, pieces)
+    )(place, picks, q, pieces, state, summary)
 
 
 def hold_kernel(after_ref, low_ref, high_ref, low_out, high_out):

time: 130 us -> 128 us (0.985)
  local copies, waits for them, and re-layouts: 14.6 us -> 11.1 us
  Pallas kernels: 33.1 us -> 35.6 us
  waiting for transfers between devices: 26.1 us -> 24.6 us
    unnamed x57 -> x51, local copies, waits for them, and re-layouts: 10.6 us -> 7.2 us
    pallas_call x1, Pallas kernels: 10.5 us -> 13 us  [far_attention(): pl.pallas_call(far_kernel, grid_spec=pltpu.PrefetchScalarGridSpec(num_sca...]
    ppermute x18, waiting for transfers between devices: 16.8 us -> 15.2 us  [shift(): return lax.ppermute(x, axis, [(i, (i + by) % size) for i in range(size)])]
  transfers between devices with their start and end apart: 25 -> 25, of which waited for: 13 -> 14; matrix products, arithmetic and copies ran while one was open for 1% -> 1% of each run, Pallas kernels for 15% -> 17%
where the time goes in v1:
time: 128 us
  starting transfers between devices  43 us (34%)
  Pallas kernels  35.6 us (28%)
  waiting for transfers between devices  24.6 us (19%)
  blocking collectives  12.9 us (10%)
  local copies, waits for them, and re-layouts  11.1 us (9%)
    ppermute x18, starting transfers between devices, shift(): return lax.ppermute(x, axis, [(i, (i + by) % size) for i in range(size)])  21.7 us
    all_to_all x2, starting transfers between devices, to_plane(): return lax.all_to_all(x, ('y', 'c'), 0, 0, tiled=True)  16.5 us
    ppermute x18, waiting for transfers between devices, shift(): return lax.ppermute(x, axis, [(i, (i + by) % size) for i in range(size)])  15.2 us
    pallas_call x1, Pallas kernels, far_attention(): pl.pallas_call(far_kernel, grid_spec=pltpu.PrefetchScalarGridSpec(num_sca...  13 us
    all_to_all x1, blocking collectives, per_device(): lax.all_to_all(attended.reshape(NX, TILE, QPK * HD), 'x', 0, 0, tiled=True)  12.9 us
    all_to_all x2, waiting for transfers between devices, to_plane(): return lax.all_to_all(x, ('y', 'c'), 0, 0, tiled=True)  9.4 us
    pallas_call x1, Pallas kernels, project(): pl.pallas_call(project_kernel, grid_spec=pltpu.PrefetchScalarGridSpec(num...  7.56 us
    unnamed x51, local copies, waits for them, and re-layouts  7.2 us
  transfers between devices with their start and end apart: 25, of which 14 were waited for; matrix products, arithmetic and copies ran while one was open for 1% of the time, Pallas kernels for 17%

profile of v1, /device:TPU:1, one launch (start us, length us, event | category | flops | bytes accessed | tf_op | source)
XLA Modules:
  0.0 127.6 jit_solution(16408789269199236054)
XLA Ops:
  0.0 3.2 %constant_dynamic-slice_fusion = bf16[256,4096]{1,0:T(8,128)(2,1)} fusion(bf16[512,4096]{1,0:T(8,128)(2,1)} %w0.1, s32[]{:T(128)S(6)} %select_n.7), kind=kLoop, calls=%fused_computation | loop fusion | bytes 4194308 | tf_op jit(solution)/shard_map/dynamic_slice | solution.py:463
  3.2 2.0 %collective-permute-start.15 = (bf16[256,4096]{1,0:T(8,128)(2,1)}, bf16[256,4096]{1,0:T(8,128)(2,1)S(1)}, u32[]{:S(2)}, u32[]{:S(2)}) collective-permute-start(bf16[256,4096]{1,0:T(8,128)(2,1)} %constant_dynamic-slice_fusion), channel_id=1, source_target_pairs={{0,1},{1,2},{2,3},{3,0},{4,5},{5,6},{6,7},{7,4},{8,9},{9,10},{10,1... | collective-permute-start | bytes 6291464 | tf_op jit(solution)/shard_map/ppermute | solution.py:447
  7.4 6.5 %all-to-all-start = ((bf16[8,80,256]{2,1,0:T(8,128)(2,1)}), bf16[8,80,256]{2,1,0:T(8,128)(2,1)S(1)}, u32[]{:S(2)}, u32[]{:S(2)}) async-start(bf16[8,80,256]{2,1,0:T(8,128)(2,1)} %get-tuple-element.20), calls=%async_computation | async-start | bytes 655360 | tf_op jit(solution)/shard_map/all_to_all | solution.py:455
  13.9 3.5 %collective-permute-start = (bf16[512,256]{1,0:T(8,128)(2,1)S(1)}, bf16[512,256]{1,0:T(8,128)(2,1)S(1)}, u32[]{:S(2)}, u32[]{:S(2)}) collective-permute-start(bf16[512,256]{1,0:T(8,128)(2,1)S(1)} %get-tuple-element.18), channel_id=1, source_target_pairs={{0,4},{4,8},{8,12},{12,16},{16,20},{20,24},{24,28},{28,32},{32,36}... | collective-permute-start | bytes 786440 | tf_op jit(solution)/shard_map/ppermute | solution.py:469
  17.4 3.6 %all-to-all-done.msg_ref = bf16[8,80,256]{2,1,0:T(8,128)(2,1)S(1)} async-done(((bf16[8,80,256]{2,1,0:T(8,128)(2,1)}), bf16[8,80,256]{2,1,0:T(8,128)(2,1)S(1)}, u32[]{:S(2)}, u32[]{:S(2)}) %all-to-all-start) | async-done | bytes 327712 | tf_op jit(solution)/shard_map/all_to_all | solution.py:455
  21.1 1.9 %collective-permute-start.1 = (bf16[272,256]{1,0:T(8,128)(2,1)S(1)}, bf16[272,256]{1,0:T(8,128)(2,1)S(1)}, u32[]{:S(2)}, u32[]{:S(2)}) collective-permute-start(bf16[272,256]{1,0:T(8,128)(2,1)S(1)} %get-tuple-element.21.refs_0_), channel_id=1, source_target_pairs={{0,32},{32,64},{64,96},{96,128},{128,160},{160,192},{192,224},{224... | collective-permute-start | bytes 417800 | tf_op jit(solution)/shard_map/ppermute | solution.py:447
  23.0 1.6 %collective-permute-start.2 = (bf16[272,256]{1,0:T(8,128)(2,1)S(1)}, bf16[272,256]{1,0:T(8,128)(2,1)S(1)}, u32[]{:S(2)}, u32[]{:S(2)}) collective-permute-start(bf16[272,256]{1,0:T(8,128)(2,1)S(1)} %get-tuple-element.22.refs_1_), channel_id=1, source_target_pairs={{0,32},{32,64},{64,96},{96,128},{128,160},{160,192},{192,224},{224... | collective-permute-start | bytes 417800 | tf_op jit(solution)/shard_map/ppermute | solution.py:447
  24.7 2.5 %collective-permute-start.8 = (bf16[272,256]{1,0:T(8,128)(2,1)S(1)}, bf16[272,256]{1,0:T(8,128)(2,1)S(1)}, u32[]{:S(2)}, u32[]{:S(2)}) collective-permute-start(bf16[272,256]{1,0:T(8,128)(2,1)S(1)} %get-tuple-element.22.refs_1_), channel_id=1, source_target_pairs={{0,224},{32,0},{64,32},{96,64},{128,96},{160,128},{192,160},{224,1... | collective-permute-start | bytes 417800 | tf_op jit(solution)/shard_map/ppermute | solution.py:447
  27.2 2.5 %collective-permute-done.1.refs_2_ = bf16[272,256]{1,0:T(8,128)(2,1)S(1)} collective-permute-done((bf16[272,256]{1,0:T(8,128)(2,1)S(1)}, bf16[272,256]{1,0:T(8,128)(2,1)S(1)}, u32[]{:S(2)}, u32[]{:S(2)}) %collective-permute-start.1) | collective-permute-done | bytes 139296 | tf_op jit(solution)/shard_map/ppermute | solution.py:447
  32.4 1.6 %collective-permute-done.12.refs_14_ = bf16[272,256]{1,0:T(8,128)(2,1)S(1)} collective-permute-done((bf16[272,256]{1,0:T(8,128)(2,1)S(1)}, bf16[272,256]{1,0:T(8,128)(2,1)S(1)}, u32[]{:S(2)}, u32[]{:S(2)}) %collective-permute-start.12) | collective-permute-done | bytes 139296 | tf_op jit(solution)/shard_map/ppermute | solution.py:447
  34.0 3.3 %collective-permute-start.9 = (bf16[272,256]{1,0:T(8,128)(2,1)S(1)}, bf16[272,256]{1,0:T(8,128)(2,1)S(1)}, u32[]{:S(2)}, u32[]{:S(2)}) collective-permute-start(bf16[272,256]{1,0:T(8,128)(2,1)S(1)} %collective-permute-done.8.refs_15_), channel_id=1, source_target_pairs={{0,224},{32,0},{64,32},{96,64},{128,96},{160,128},{192,160},{224,1... | collective-permute-start | bytes 417800 | tf_op jit(solution)/shard_map/ppermute | solution.py:447
  39.4 2.7 %collective-permute-done.13.refs_12_ = bf16[272,256]{1,0:T(8,128)(2,1)} collective-permute-done((bf16[272,256]{1,0:T(8,128)(2,1)S(1)}, bf16[272,256]{1,0:T(8,128)(2,1)}, u32[]{:S(2)}, u32[]{:S(2)}) %collective-permute-start.13) | collective-permute-done | bytes 139296 | tf_op jit(solution)/shard_map/ppermute | solution.py:447
  42.0 2.2 %collective-permute-start.10 = (bf16[272,256]{1,0:T(8,128)(2,1)S(1)}, bf16[272,256]{1,0:T(8,128)(2,1)}, u32[]{:S(2)}, u32[]{:S(2)}) collective-permute-start(bf16[272,256]{1,0:T(8,128)(2,1)S(1)} %collective-permute-done.9.refs_13_), channel_id=1, source_target_pairs={{0,224},{32,0},{64,32},{96,64},{128,96},{160,128},{192,160},{224,1... | collective-permute-start | bytes 417800 | tf_op jit(solution)/shard_map/ppermute | solution.py:447
  47.4 2.3 %collective-permute-start.11 = (bf16[272,256]{1,0:T(8,128)(2,1)}, bf16[272,256]{1,0:T(8,128)(2,1)}, u32[]{:S(2)}, u32[]{:S(2)}) collective-permute-start(bf16[272,256]{1,0:T(8,128)(2,1)} %collective-permute-done.10.refs_11_), channel_id=1, source_target_pairs={{0,224},{32,0},{64,32},{96,64},{128,96},{160,128},{192,160},{224,1... | collective-permute-start | bytes 417800 | tf_op jit(solution)/shard_map/ppermute | solution.py:447
  51.7 1.7 %collective-permute-done.11.refs_9_ = bf16[272,256]{1,0:T(8,128)(2,1)} collective-permute-done((bf16[272,256]{1,0:T(8,128)(2,1)}, bf16[272,256]{1,0:T(8,128)(2,1)}, u32[]{:S(2)}, u32[]{:S(2)}) %collective-permute-start.11) | collective-permute-done | bytes 139296 | tf_op jit(solution)/shard_map/ppermute | solution.py:447
  54.8 6.7 %pick_pieces.1 = (bf16[256,4096]{1,0:T(8,128)(2,1)}, bf16[256,4096]{1,0:T(8,128)(2,1)}, bf16[3072,256]{1,0:T(8,128)(2,1)}, bf16[128,4096]{1,0:T(8,128)(2,1)}, bf16[128,4096]{1,0:T(8,128)(2,1)}) custom-call(s32[5]{0:T(128)} %stack.23.place_ref, s32[8,7]{1,0:T(8,128)} %bitcast.16, ...), custom_call_target="tpu_custom_call", output_to_operand_aliasing={{0}: (19, {}), {1}: (20, {})} | custom-call | bytes 1048576 | tf_op jit(solution)/shard_map/pick_pieces/pallas_call | solution.py:137
  61.6 10.0 %all-to-all-start.1 = ((bf16[8,384,256]{2,1,0:T(8,128)(2,1)}), bf16[8,384,256]{2,1,0:T(8,128)(2,1)}, u32[]{:S(2)}, u32[]{:S(2)}) async-start(bf16[8,384,256]{2,1,0:T(8,128)(2,1)} %bitcast.15), calls=%async_computation.1 | async-start | bytes 3145728 | tf_op jit(solution)/shard_map/all_to_all | solution.py:455
  72.6 1.7 %collective-permute-start.18 = (bf16[128,4096]{1,0:T(8,128)(2,1)}, bf16[128,4096]{1,0:T(8,128)(2,1)}, u32[]{:S(2)}, u32[]{:S(2)}) collective-permute-start(bf16[128,4096]{1,0:T(8,128)(2,1)} %get-tuple-element.28), channel_id=1, source_target_pairs={{0,3},{1,0},{2,1},{3,2},{4,7},{5,4},{6,5},{7,6},{8,11},{9,8},{10,9... | collective-permute-start | bytes 3145736 | tf_op jit(solution)/shard_map/ppermute | solution.py:447
  77.0 3.6 %near_attention.1 = (bf16[2048,128]{1,0:T(8,128)(2,1)S(1)}, f32[2048,256]{1,0:T(8,128)S(1)}) custom-call(s32[5]{0:T(128)S(1)} %copy-done.15, bf16[512,512]{1,0:T(8,128)(2,1)S(1)} %copy-done.10, bf16[512,128]{1,0:T(8,128)(2,1)S(1)} %copy-done.12, bf16[512,128]{1,0:T(8,128)(2,1)S(1)} %copy-done.14, bf16[512,256]{1,0:T(8,128)(2,1)S(1)} %copy-done.7), custom_call_target="tpu_custom_call" | custom-call | flops 1048576 | bytes 1048576 | tf_op jit(solution)/shard_map/near_attention/pallas_call | solution.py:205
  82.8 3.8 %summary_attention.1.summary_hbm = f32[2048,128]{1,0:T(8,128)} custom-call(s32[5]{0:T(128)} %stack.23.place_ref, bf16[2048,128]{1,0:T(8,128)(2,1)} %copy-done.5, bf16[272,256]{1,0:T(8,128)(2,1)} %copy-done.8, bf16[272,256]{1,0:T(8,128)(2,1)} %copy-done.9, bf16[272,256]{1,0:T(8,128)(2,1)} %copy-done.17, bf16[272,256]{1,0:T(8,128)(2,1)} %copy-done.18, ...), custom_call_target="tpu_custom_call" | custom-call | flops 1048576 | bytes 1048576 | tf_op jit(solution)/shard_map/summary_attention/pallas_call | solution.py:263
  86.6 5.8 %all-to-all-done.1 = bf16[8,384,256]{2,1,0:T(8,128)(2,1)} async-done(((bf16[8,384,256]{2,1,0:T(8,128)(2,1)}), bf16[8,384,256]{2,1,0:T(8,128)(2,1)}, u32[]{:S(2)}, u32[]{:S(2)}) %all-to-all-start.1) | async-done | bytes 1572896 | tf_op jit(solution)/shard_map/all_to_all | solution.py:455
  92.4 13.0 %far_attention.1.after_ref = bf16[512,512]{1,0:T(8,128)(2,1)} custom-call(s32[5]{0:T(128)} %stack.23.place_ref, s32[8,7]{1,0:T(8,128)} %bitcast.17, bf16[2048,128]{1,0:T(8,128)(2,1)} %copy-done.5, bf16[3072,256]{1,0:T(8,128)(2,1)} %bitcast.7.pieces_ref, f32[2048,256]{1,0:T(8,128)} %copy-done.4, f32[2048,128]{1,0:T(8,128)} %summary_attention.1.summary_hbm), custom_call_target="tpu_custom_call" | custom-call | flops 1048576 | bytes 1048576 | tf_op jit(solution)/shard_map/far_attention/pallas_call | solution.py:372
  107.0 12.9 %all_to_all.21 = bf16[4,128,512]{2,1,0:T(8,128)(2,1)S(1)} all-to-all(bf16[4,128,512]{2,1,0:T(8,128)(2,1)S(1)} %bitcast.12), channel_id=1, replica_groups=mesh['z'=8,'y'=4,'c'=2,'x'=4] {'x'}, dimensions={0} | all-to-all | bytes 1048576 | tf_op jit(solution)/shard_map/all_to_all | solution.py:487
  120.0 7.6 %project.1 = bf16[128,4096]{1,0:T(8,128)(2,1)} custom-call(s32[5]{0:T(128)S(1)} %copy-done.16, bf16[128,2048]{1,0:T(8,128)(2,1)S(1)} %bitcast.13, bf16[512,4096]{1,0:T(8,128)(2,1)} %w0.1, bf16[256,4096]{1,0:T(8,128)(2,1)S(1)} %copy-done.2, bf16[256,4096]{1,0:T(8,128)(2,1)} %get-tuple-element.26.refs_1_, bf16[128,4096]{1,0:T(8,128)(2,1)S(1)} %get-tuple-element.29.refs_2_, ...), custom_call_target="tpu_custom_call" | custom-call | flops 1048576 | bytes 1048576 | tf_op jit(solution)/shard_map/project/pallas_call | solution.py:430
  (90 shorter events, 20.9 us)
Async XLA Ops:
  3.2 50.2 %collective-permute-start.15 = (bf16[256,4096]{1,0:T(8,128)(2,1)}, bf16[256,4096]{1,0:T(8,128)(2,1)S(1)}, u32[]{:S(2)}, u32[]{:S(2)}) collective-permute-start(bf16[256,4096]{1,0:T(8,128)(2,1)} %constant_dynamic-slice_fusion), channel_id=1, source_target_pairs={{0,1},{1,2},{2,3},{3,0},{4,5},{5,6},{6,7},{7,4},{8,9},{9,10},{10,1... | collective-permute-start | bytes 6291464 | tf_op jit(solution)/shard_map/ppermute | solution.py:447
  5.3 48.2 %collective-permute-start.16 = (bf16[256,4096]{1,0:T(8,128)(2,1)}, bf16[256,4096]{1,0:T(8,128)(2,1)}, u32[]{:S(2)}, u32[]{:S(2)}) collective-permute-start(bf16[256,4096]{1,0:T(8,128)(2,1)} %constant_dynamic-slice_fusion), channel_id=1, source_target_pairs={{0,3},{1,0},{2,1},{3,2},{4,7},{5,4},{6,5},{7,6},{8,11},{9,8},{10,9... | collective-permute-start | bytes 6291464 | tf_op jit(solution)/shard_map/ppermute | solution.py:447
  7.4 13.7 %all-to-all-start = ((bf16[8,80,256]{2,1,0:T(8,128)(2,1)}), bf16[8,80,256]{2,1,0:T(8,128)(2,1)S(1)}, u32[]{:S(2)}, u32[]{:S(2)}) async-start(bf16[8,80,256]{2,1,0:T(8,128)(2,1)} %get-tuple-element.20), calls=%async_computation | async-start | bytes 655360 | tf_op jit(solution)/shard_map/all_to_all | solution.py:455
  13.9 10.8 %collective-permute-start = (bf16[512,256]{1,0:T(8,128)(2,1)S(1)}, bf16[512,256]{1,0:T(8,128)(2,1)S(1)}, u32[]{:S(2)}, u32[]{:S(2)}) collective-permute-start(bf16[512,256]{1,0:T(8,128)(2,1)S(1)} %get-tuple-element.18), channel_id=1, source_target_pairs={{0,4},{4,8},{8,12},{12,16},{16,20},{20,24},{24,28},{28,32},{32,36}... | collective-permute-start | bytes 786440 | tf_op jit(solution)/shard_map/ppermute | solution.py:469
  21.1 8.6 %collective-permute-start.1 = (bf16[272,256]{1,0:T(8,128)(2,1)S(1)}, bf16[272,256]{1,0:T(8,128)(2,1)S(1)}, u32[]{:S(2)}, u32[]{:S(2)}) collective-permute-start(bf16[272,256]{1,0:T(8,128)(2,1)S(1)} %get-tuple-element.21.refs_0_), channel_id=1, source_target_pairs={{0,32},{32,64},{64,96},{96,128},{128,160},{160,192},{192,224},{224... | collective-permute-start | bytes 417800 | tf_op jit(solution)/shard_map/ppermute | solution.py:447
  23.0 9.3 %collective-permute-start.2 = (bf16[272,256]{1,0:T(8,128)(2,1)S(1)}, bf16[272,256]{1,0:T(8,128)(2,1)S(1)}, u32[]{:S(2)}, u32[]{:S(2)}) collective-permute-start(bf16[272,256]{1,0:T(8,128)(2,1)S(1)} %get-tuple-element.22.refs_1_), channel_id=1, source_target_pairs={{0,32},{32,64},{64,96},{96,128},{128,160},{160,192},{192,224},{224... | collective-permute-start | bytes 417800 | tf_op jit(solution)/shard_map/ppermute | solution.py:447
  24.7 7.6 %collective-permute-start.8 = (bf16[272,256]{1,0:T(8,128)(2,1)S(1)}, bf16[272,256]{1,0:T(8,128)(2,1)S(1)}, u32[]{:S(2)}, u32[]{:S(2)}) collective-permute-start(bf16[272,256]{1,0:T(8,128)(2,1)S(1)} %get-tuple-element.22.refs_1_), channel_id=1, source_target_pairs={{0,224},{32,0},{64,32},{96,64},{128,96},{160,128},{192,160},{224,1... | collective-permute-start | bytes 417800 | tf_op jit(solution)/shard_map/ppermute | solution.py:447
  32.3 5.4 %collective-permute-start.3 = (bf16[272,256]{1,0:T(8,128)(2,1)S(1)}, bf16[272,256]{1,0:T(8,128)(2,1)S(1)}, u32[]{:S(2)}, u32[]{:S(2)}) collective-permute-start(bf16[272,256]{1,0:T(8,128)(2,1)S(1)} %collective-permute-done.1.refs_2_), channel_id=1, source_target_pairs={{0,32},{32,64},{64,96},{96,128},{128,160},{160,192},{192,224},{224... | collective-permute-start | bytes 417800 | tf_op jit(solution)/shard_map/ppermute | solution.py:447
  32.3 6.9 %collective-permute-start.4 = (bf16[272,256]{1,0:T(8,128)(2,1)S(1)}, bf16[272,256]{1,0:T(8,128)(2,1)S(1)}, u32[]{:S(2)}, u32[]{:S(2)}) collective-permute-start(bf16[272,256]{1,0:T(8,128)(2,1)S(1)} %collective-permute-done.2.refs_3_), channel_id=1, source_target_pairs={{0,32},{32,64},{64,96},{96,128},{128,160},{160,192},{192,224},{224... | collective-permute-start | bytes 417800 | tf_op jit(solution)/shard_map/ppermute | solution.py:447
  34.0 5.3 %collective-permute-start.9 = (bf16[272,256]{1,0:T(8,128)(2,1)S(1)}, bf16[272,256]{1,0:T(8,128)(2,1)S(1)}, u32[]{:S(2)}, u32[]{:S(2)}) collective-permute-start(bf16[272,256]{1,0:T(8,128)(2,1)S(1)} %collective-permute-done.8.refs_15_), channel_id=1, source_target_pairs={{0,224},{32,0},{64,32},{96,64},{128,96},{160,128},{192,160},{224,1... | collective-permute-start | bytes 417800 | tf_op jit(solution)/shard_map/ppermute | solution.py:447
  37.7 4.3 %collective-permute-start.13 = (bf16[272,256]{1,0:T(8,128)(2,1)S(1)}, bf16[272,256]{1,0:T(8,128)(2,1)}, u32[]{:S(2)}, u32[]{:S(2)}) collective-permute-start(bf16[272,256]{1,0:T(8,128)(2,1)S(1)} %collective-permute-done.12.refs_14_), channel_id=1, source_target_pairs={{0,224},{32,0},{64,32},{96,64},{128,96},{160,128},{192,160},{224,1... | collective-permute-start | bytes 417800 | tf_op jit(solution)/shard_map/ppermute | solution.py:447
  39.2 5.4 %collective-permute-start.5 = (bf16[272,256]{1,0:T(8,128)(2,1)S(1)}, bf16[272,256]{1,0:T(8,128)(2,1)}, u32[]{:S(2)}, u32[]{:S(2)}) collective-permute-start(bf16[272,256]{1,0:T(8,128)(2,1)S(1)} %collective-permute-done.3.refs_4_), channel_id=1, source_target_pairs={{0,32},{32,64},{64,96},{96,128},{128,160},{160,192},{192,224},{224... | collective-permute-start | bytes 417800 | tf_op jit(solution)/shard_map/ppermute | solution.py:447
  39.4 6.7 %collective-permute-start.6 = (bf16[272,256]{1,0:T(8,128)(2,1)S(1)}, bf16[272,256]{1,0:T(8,128)(2,1)S(1)}, u32[]{:S(2)}, u32[]{:S(2)}) collective-permute-start(bf16[272,256]{1,0:T(8,128)(2,1)S(1)} %collective-permute-done.4.refs_5_), channel_id=1, source_target_pairs={{0,32},{32,64},{64,96},{96,128},{128,160},{160,192},{192,224},{224... | collective-permute-start | bytes 417800 | tf_op jit(solution)/shard_map/ppermute | solution.py:447
  42.0 5.4 %collective-permute-start.10 = (bf16[272,256]{1,0:T(8,128)(2,1)S(1)}, bf16[272,256]{1,0:T(8,128)(2,1)}, u32[]{:S(2)}, u32[]{:S(2)}) collective-permute-start(bf16[272,256]{1,0:T(8,128)(2,1)S(1)} %collective-permute-done.9.refs_13_), channel_id=1, source_target_pairs={{0,224},{32,0},{64,32},{96,64},{128,96},{160,128},{192,160},{224,1... | collective-permute-start | bytes 417800 | tf_op jit(solution)/shard_map/ppermute | solution.py:447
  44.6 6.4 %collective-permute-start.14 = (bf16[272,256]{1,0:T(8,128)(2,1)}, bf16[272,256]{1,0:T(8,128)(2,1)}, u32[]{:S(2)}, u32[]{:S(2)}) collective-permute-start(bf16[272,256]{1,0:T(8,128)(2,1)} %collective-permute-done.13.refs_12_), channel_id=1, source_target_pairs={{0,224},{32,0},{64,32},{96,64},{128,96},{160,128},{192,160},{224,1... | collective-permute-start | bytes 417800 | tf_op jit(solution)/shard_map/ppermute | solution.py:447
  46.1 5.6 %collective-permute-start.7 = (bf16[272,256]{1,0:T(8,128)(2,1)}, bf16[272,256]{1,0:T(8,128)(2,1)}, u32[]{:S(2)}, u32[]{:S(2)}) collective-permute-start(bf16[272,256]{1,0:T(8,128)(2,1)} %collective-permute-done.5.refs_6_), channel_id=1, source_target_pairs={{0,32},{32,64},{64,96},{96,128},{128,160},{160,192},{192,224},{224... | collective-permute-start | bytes 417800 | tf_op jit(solution)/shard_map/ppermute | solution.py:447
  47.4 6.1 %collective-permute-start.11 = (bf16[272,256]{1,0:T(8,128)(2,1)}, bf16[272,256]{1,0:T(8,128)(2,1)}, u32[]{:S(2)}, u32[]{:S(2)}) collective-permute-start(bf16[272,256]{1,0:T(8,128)(2,1)} %collective-permute-done.10.refs_11_), channel_id=1, source_target_pairs={{0,224},{32,0},{64,32},{96,64},{128,96},{160,128},{192,160},{224,1... | collective-permute-start | bytes 417800 | tf_op jit(solution)/shard_map/ppermute | solution.py:447
  61.6 30.9 %all-to-all-start.1 = ((bf16[8,384,256]{2,1,0:T(8,128)(2,1)}), bf16[8,384,256]{2,1,0:T(8,128)(2,1)}, u32[]{:S(2)}, u32[]{:S(2)}) async-start(bf16[8,384,256]{2,1,0:T(8,128)(2,1)} %bitcast.15), calls=%async_computation.1 | async-start | bytes 3145728 | tf_op jit(solution)/shard_map/all_to_all | solution.py:455
  71.6 33.8 %collective-permute-start.17 = (bf16[128,4096]{1,0:T(8,128)(2,1)}, bf16[128,4096]{1,0:T(8,128)(2,1)S(1)}, u32[]{:S(2)}, u32[]{:S(2)}) collective-permute-start(bf16[128,4096]{1,0:T(8,128)(2,1)} %get-tuple-element.27), channel_id=1, source_target_pairs={{0,1},{1,2},{2,3},{3,0},{4,5},{5,6},{6,7},{7,4},{8,9},{9,10},{10,1... | collective-permute-start | bytes 3145736 | tf_op jit(solution)/shard_map/ppermute | solution.py:447
  72.6 32.9 %collective-permute-start.18 = (bf16[128,4096]{1,0:T(8,128)(2,1)}, bf16[128,4096]{1,0:T(8,128)(2,1)}, u32[]{:S(2)}, u32[]{:S(2)}) collective-permute-start(bf16[128,4096]{1,0:T(8,128)(2,1)} %get-tuple-element.28), channel_id=1, source_target_pairs={{0,3},{1,0},{2,1},{3,2},{4,7},{5,4},{6,5},{7,6},{8,11},{9,8},{10,9... | collective-permute-start | bytes 3145736 | tf_op jit(solution)/shard_map/ppermute | solution.py:447
  74.3 45.7 %collective-permute-start.19 = (bf16[256,4096]{1,0:T(8,128)(2,1)S(1)}, bf16[256,4096]{1,0:T(8,128)(2,1)}, u32[]{:S(2)}, u32[]{:S(2)}) collective-permute-start(bf16[256,4096]{1,0:T(8,128)(2,1)S(1)} %copy-done.2), channel_id=1, source_target_pairs={{0,4},{4,0},{1,5},{5,1},{2,6},{6,2},{3,7},{7,3},{8,12},{12,8},{9,1... | collective-permute-start | bytes 6291464 | tf_op jit(solution)/shard_map/ppermute | solution.py:451
  75.0 44.9 %collective-permute-start.20 = (bf16[256,4096]{1,0:T(8,128)(2,1)}, bf16[256,4096]{1,0:T(8,128)(2,1)}, u32[]{:S(2)}, u32[]{:S(2)}) collective-permute-start(bf16[256,4096]{1,0:T(8,128)(2,1)} %get-tuple-element.26.refs_1_), channel_id=1, source_target_pairs={{0,4},{4,0},{1,5},{5,1},{2,6},{6,2},{3,7},{7,3},{8,12},{12,8},{9,1... | collective-permute-start | bytes 6291464 | tf_op jit(solution)/shard_map/ppermute | solution.py:451
  106.5 13.5 %collective-permute-start.21 = (bf16[128,4096]{1,0:T(8,128)(2,1)S(1)}, bf16[128,4096]{1,0:T(8,128)(2,1)S(1)}, u32[]{:S(2)}, u32[]{:S(2)}) collective-permute-start(bf16[128,4096]{1,0:T(8,128)(2,1)S(1)} %get-tuple-element.29.refs_2_), channel_id=1, source_target_pairs={{0,4},{4,0},{1,5},{5,1},{2,6},{6,2},{3,7},{7,3},{8,12},{12,8},{9,1... | collective-permute-start | bytes 3145736 | tf_op jit(solution)/shard_map/ppermute | solution.py:451
  106.5 13.5 %collective-permute-start.22 = (bf16[128,4096]{1,0:T(8,128)(2,1)}, bf16[128,4096]{1,0:T(8,128)(2,1)S(1)}, u32[]{:S(2)}, u32[]{:S(2)}) collective-permute-start(bf16[128,4096]{1,0:T(8,128)(2,1)} %get-tuple-element.30.refs_3_), channel_id=1, source_target_pairs={{0,4},{4,0},{1,5},{5,1},{2,6},{6,2},{3,7},{7,3},{8,12},{12,8},{9,1... | collective-permute-start | bytes 3145736 | tf_op jit(solution)/shard_map/ppermute | solution.py:451
  (26 other events, 362.9 us)

commit v2 on v1

--- a/solution.py
+++ b/solution.py
@@ -123,7 +123,7 @@
 
     for copy in sides:
         copy.start()
-    lax.fori_loop(0, PIECES * PICKS, step, 0)
+    lax.fori_loop(0, PIECES * PICKS, step, 0, unroll=4)
     pltpu.make_async_copy(out, out, sem).wait()
     for copy in sides:
         copy.wait()

time: 128 us -> 127 us (level)
  no operation moved by 1% of the time
where the time goes in v2:
time: 127 us
  starting transfers between devices  43 us (34%)
  Pallas kernels  34.7 us (27%)
  waiting for transfers between devices  24.7 us (19%)
  blocking collectives  12.9 us (10%)
  local copies, waits for them, and re-layouts  11.1 us (9%)
    ppermute x18, starting transfers between devices, shift(): return lax.ppermute(x, axis, [(i, (i + by) % size) for i in range(size)])  21.7 us
    all_to_all x2, starting transfers between devices, to_plane(): return lax.all_to_all(x, ('y', 'c'), 0, 0, tiled=True)  16.5 us
    ppermute x18, waiting for transfers between devices, shift(): return lax.ppermute(x, axis, [(i, (i + by) % size) for i in range(size)])  15.2 us
    pallas_call x1, Pallas kernels, far_attention(): pl.pallas_call(far_kernel, grid_spec=pltpu.PrefetchScalarGridSpec(num_sca...  13 us
    all_to_all x1, blocking collectives, per_device(): lax.all_to_all(attended.reshape(NX, TILE, QPK * HD), 'x', 0, 0, tiled=True)  12.9 us
    all_to_all x2, waiting for transfers between devices, to_plane(): return lax.all_to_all(x, ('y', 'c'), 0, 0, tiled=True)  9.41 us
    pallas_call x1, Pallas kernels, project(): pl.pallas_call(project_kernel, grid_spec=pltpu.PrefetchScalarGridSpec(num...  7.56 us
    unnamed x51, local copies, waits for them, and re-layouts  7.2 us
  transfers between devices with their start and end apart: 25, of which 14 were waited for; matrix products, arithmetic and copies ran while one was open for 1% of the time, Pallas kernels for 17%

profile of v2, /device:TPU:1, one launch (start us, length us, event | category | flops | bytes accessed | tf_op | source)
XLA Modules:
  0.0 126.7 jit_solution(985024754887194249)
XLA Ops:
  0.0 3.2 %constant_dynamic-slice_fusion = bf16[256,4096]{1,0:T(8,128)(2,1)} fusion(bf16[512,4096]{1,0:T(8,128)(2,1)} %w0.1, s32[]{:T(128)S(6)} %select_n.7), kind=kLoop, calls=%fused_computation | loop fusion | bytes 4194308 | tf_op jit(solution)/shard_map/dynamic_slice | solution.py:463
  3.2 2.0 %collective-permute-start.15 = (bf16[256,4096]{1,0:T(8,128)(2,1)}, bf16[256,4096]{1,0:T(8,128)(2,1)S(1)}, u32[]{:S(2)}, u32[]{:S(2)}) collective-permute-start(bf16[256,4096]{1,0:T(8,128)(2,1)} %constant_dynamic-slice_fusion), channel_id=1, source_target_pairs={{0,1},{1,2},{2,3},{3,0},{4,5},{5,6},{6,7},{7,4},{8,9},{9,10},{10,1... | collective-permute-start | bytes 6291464 | tf_op jit(solution)/shard_map/ppermute | solution.py:447
  7.4 6.5 %all-to-all-start = ((bf16[8,80,256]{2,1,0:T(8,128)(2,1)}), bf16[8,80,256]{2,1,0:T(8,128)(2,1)S(1)}, u32[]{:S(2)}, u32[]{:S(2)}) async-start(bf16[8,80,256]{2,1,0:T(8,128)(2,1)} %get-tuple-element.20), calls=%async_computation | async-start | bytes 655360 | tf_op jit(solution)/shard_map/all_to_all | solution.py:455
  13.9 3.5 %collective-permute-start = (bf16[512,256]{1,0:T(8,128)(2,1)S(1)}, bf16[512,256]{1,0:T(8,128)(2,1)S(1)}, u32[]{:S(2)}, u32[]{:S(2)}) collective-permute-start(bf16[512,256]{1,0:T(8,128)(2,1)S(1)} %get-tuple-element.18), channel_id=1, source_target_pairs={{0,4},{4,8},{8,12},{12,16},{16,20},{20,24},{24,28},{28,32},{32,36}... | collective-permute-start | bytes 786440 | tf_op jit(solution)/shard_map/ppermute | solution.py:469
  17.4 3.6 %all-to-all-done.msg_ref = bf16[8,80,256]{2,1,0:T(8,128)(2,1)S(1)} async-done(((bf16[8,80,256]{2,1,0:T(8,128)(2,1)}), bf16[8,80,256]{2,1,0:T(8,128)(2,1)S(1)}, u32[]{:S(2)}, u32[]{:S(2)}) %all-to-all-start) | async-done | bytes 327712 | tf_op jit(solution)/shard_map/all_to_all | solution.py:455
  21.1 1.9 %collective-permute-start.1 = (bf16[272,256]{1,0:T(8,128)(2,1)S(1)}, bf16[272,256]{1,0:T(8,128)(2,1)S(1)}, u32[]{:S(2)}, u32[]{:S(2)}) collective-permute-start(bf16[272,256]{1,0:T(8,128)(2,1)S(1)} %get-tuple-element.21.refs_0_), channel_id=1, source_target_pairs={{0,32},{32,64},{64,96},{96,128},{128,160},{160,192},{192,224},{224... | collective-permute-start | bytes 417800 | tf_op jit(solution)/shard_map/ppermute | solution.py:447
  23.0 1.6 %collective-permute-start.2 = (bf16[272,256]{1,0:T(8,128)(2,1)S(1)}, bf16[272,256]{1,0:T(8,128)(2,1)S(1)}, u32[]{:S(2)}, u32[]{:S(2)}) collective-permute-start(bf16[272,256]{1,0:T(8,128)(2,1)S(1)} %get-tuple-element.22.refs_1_), channel_id=1, source_target_pairs={{0,32},{32,64},{64,96},{96,128},{128,160},{160,192},{192,224},{224... | collective-permute-start | bytes 417800 | tf_op jit(solution)/shard_map/ppermute | solution.py:447
  24.7 2.5 %collective-permute-start.8 = (bf16[272,256]{1,0:T(8,128)(2,1)S(1)}, bf16[272,256]{1,0:T(8,128)(2,1)S(1)}, u32[]{:S(2)}, u32[]{:S(2)}) collective-permute-start(bf16[272,256]{1,0:T(8,128)(2,1)S(1)} %get-tuple-element.22.refs_1_), channel_id=1, source_target_pairs={{0,224},{32,0},{64,32},{96,64},{128,96},{160,128},{192,160},{224,1... | collective-permute-start | bytes 417800 | tf_op jit(solution)/shard_map/ppermute | solution.py:447
  27.2 2.5 %collective-permute-done.1.refs_2_ = bf16[272,256]{1,0:T(8,128)(2,1)S(1)} collective-permute-done((bf16[272,256]{1,0:T(8,128)(2,1)S(1)}, bf16[272,256]{1,0:T(8,128)(2,1)S(1)}, u32[]{:S(2)}, u32[]{:S(2)}) %collective-permute-start.1) | collective-permute-done | bytes 139296 | tf_op jit(solution)/shard_map/ppermute | solution.py:447
  32.4 1.6 %collective-permute-done.12.refs_14_ = bf16[272,256]{1,0:T(8,128)(2,1)S(1)} collective-permute-done((bf16[272,256]{1,0:T(8,128)(2,1)S(1)}, bf16[272,256]{1,0:T(8,128)(2,1)S(1)}, u32[]{:S(2)}, u32[]{:S(2)}) %collective-permute-start.12) | collective-permute-done | bytes 139296 | tf_op jit(solution)/shard_map/ppermute | solution.py:447
  34.0 3.3 %collective-permute-start.9 = (bf16[272,256]{1,0:T(8,128)(2,1)S(1)}, bf16[272,256]{1,0:T(8,128)(2,1)S(1)}, u32[]{:S(2)}, u32[]{:S(2)}) collective-permute-start(bf16[272,256]{1,0:T(8,128)(2,1)S(1)} %collective-permute-done.8.refs_15_), channel_id=1, source_target_pairs={{0,224},{32,0},{64,32},{96,64},{128,96},{160,128},{192,160},{224,1... | collective-permute-start | bytes 417800 | tf_op jit(solution)/shard_map/ppermute | solution.py:447
  39.4 2.7 %collective-permute-done.13.refs_12_ = bf16[272,256]{1,0:T(8,128)(2,1)} collective-permute-done((bf16[272,256]{1,0:T(8,128)(2,1)S(1)}, bf16[272,256]{1,0:T(8,128)(2,1)}, u32[]{:S(2)}, u32[]{:S(2)}) %collective-permute-start.13) | collective-permute-done | bytes 139296 | tf_op jit(solution)/shard_map/ppermute | solution.py:447
  42.0 2.2 %collective-permute-start.10 = (bf16[272,256]{1,0:T(8,128)(2,1)S(1)}, bf16[272,256]{1,0:T(8,128)(2,1)}, u32[]{:S(2)}, u32[]{:S(2)}) collective-permute-start(bf16[272,256]{1,0:T(8,128)(2,1)S(1)} %collective-permute-done.9.refs_13_), channel_id=1, source_target_pairs={{0,224},{32,0},{64,32},{96,64},{128,96},{160,128},{192,160},{224,1... | collective-permute-start | bytes 417800 | tf_op jit(solution)/shard_map/ppermute | solution.py:447
  47.4 2.3 %collective-permute-start.11 = (bf16[272,256]{1,0:T(8,128)(2,1)}, bf16[272,256]{1,0:T(8,128)(2,1)}, u32[]{:S(2)}, u32[]{:S(2)}) collective-permute-start(bf16[272,256]{1,0:T(8,128)(2,1)} %collective-permute-done.10.refs_11_), channel_id=1, source_target_pairs={{0,224},{32,0},{64,32},{96,64},{128,96},{160,128},{192,160},{224,1... | collective-permute-start | bytes 417800 | tf_op jit(solution)/shard_map/ppermute | solution.py:447
  51.7 1.7 %collective-permute-done.11.refs_9_ = bf16[272,256]{1,0:T(8,128)(2,1)} collective-permute-done((bf16[272,256]{1,0:T(8,128)(2,1)}, bf16[272,256]{1,0:T(8,128)(2,1)}, u32[]{:S(2)}, u32[]{:S(2)}) %collective-permute-start.11) | collective-permute-done | bytes 139296 | tf_op jit(solution)/shard_map/ppermute | solution.py:447
  54.8 5.9 %pick_pieces.1 = (bf16[256,4096]{1,0:T(8,128)(2,1)}, bf16[256,4096]{1,0:T(8,128)(2,1)}, bf16[3072,256]{1,0:T(8,128)(2,1)}, bf16[128,4096]{1,0:T(8,128)(2,1)}, bf16[128,4096]{1,0:T(8,128)(2,1)}) custom-call(s32[5]{0:T(128)} %stack.23.place_ref, s32[8,7]{1,0:T(8,128)} %bitcast.16, ...), custom_call_target="tpu_custom_call", output_to_operand_aliasing={{0}: (19, {}), {1}: (20, {})} | custom-call | bytes 1048576 | tf_op jit(solution)/shard_map/pick_pieces/pallas_call | solution.py:137
  60.7 10.0 %all-to-all-start.1 = ((bf16[8,384,256]{2,1,0:T(8,128)(2,1)}), bf16[8,384,256]{2,1,0:T(8,128)(2,1)}, u32[]{:S(2)}, u32[]{:S(2)}) async-start(bf16[8,384,256]{2,1,0:T(8,128)(2,1)} %bitcast.15), calls=%async_computation.1 | async-start | bytes 3145728 | tf_op jit(solution)/shard_map/all_to_all | solution.py:455
  71.7 1.7 %collective-permute-start.18 = (bf16[128,4096]{1,0:T(8,128)(2,1)}, bf16[128,4096]{1,0:T(8,128)(2,1)}, u32[]{:S(2)}, u32[]{:S(2)}) collective-permute-start(bf16[128,4096]{1,0:T(8,128)(2,1)} %get-tuple-element.28), channel_id=1, source_target_pairs={{0,3},{1,0},{2,1},{3,2},{4,7},{5,4},{6,5},{7,6},{8,11},{9,8},{10,9... | collective-permute-start | bytes 3145736 | tf_op jit(solution)/shard_map/ppermute | solution.py:447
  76.1 3.7 %near_attention.1 = (bf16[2048,128]{1,0:T(8,128)(2,1)S(1)}, f32[2048,256]{1,0:T(8,128)S(1)}) custom-call(s32[5]{0:T(128)S(1)} %copy-done.15, bf16[512,512]{1,0:T(8,128)(2,1)S(1)} %copy-done.10, bf16[512,128]{1,0:T(8,128)(2,1)S(1)} %copy-done.12, bf16[512,128]{1,0:T(8,128)(2,1)S(1)} %copy-done.14, bf16[512,256]{1,0:T(8,128)(2,1)S(1)} %copy-done.7), custom_call_target="tpu_custom_call" | custom-call | flops 1048576 | bytes 1048576 | tf_op jit(solution)/shard_map/near_attention/pallas_call | solution.py:205
  82.0 3.8 %summary_attention.1.summary_hbm = f32[2048,128]{1,0:T(8,128)} custom-call(s32[5]{0:T(128)} %stack.23.place_ref, bf16[2048,128]{1,0:T(8,128)(2,1)} %copy-done.5, bf16[272,256]{1,0:T(8,128)(2,1)} %copy-done.8, bf16[272,256]{1,0:T(8,128)(2,1)} %copy-done.9, bf16[272,256]{1,0:T(8,128)(2,1)} %copy-done.17, bf16[272,256]{1,0:T(8,128)(2,1)} %copy-done.18, ...), custom_call_target="tpu_custom_call" | custom-call | flops 1048576 | bytes 1048576 | tf_op jit(solution)/shard_map/summary_attention/pallas_call | solution.py:263
  85.8 5.8 %all-to-all-done.1 = bf16[8,384,256]{2,1,0:T(8,128)(2,1)} async-done(((bf16[8,384,256]{2,1,0:T(8,128)(2,1)}), bf16[8,384,256]{2,1,0:T(8,128)(2,1)}, u32[]{:S(2)}, u32[]{:S(2)}) %all-to-all-start.1) | async-done | bytes 1572896 | tf_op jit(solution)/shard_map/all_to_all | solution.py:455
  91.6 13.0 %far_attention.1.after_ref = bf16[512,512]{1,0:T(8,128)(2,1)} custom-call(s32[5]{0:T(128)} %stack.23.place_ref, s32[8,7]{1,0:T(8,128)} %bitcast.17, bf16[2048,128]{1,0:T(8,128)(2,1)} %copy-done.5, bf16[3072,256]{1,0:T(8,128)(2,1)} %bitcast.7.pieces_ref, f32[2048,256]{1,0:T(8,128)} %copy-done.4, f32[2048,128]{1,0:T(8,128)} %summary_attention.1.summary_hbm), custom_call_target="tpu_custom_call" | custom-call | flops 1048576 | bytes 1048576 | tf_op jit(solution)/shard_map/far_attention/pallas_call | solution.py:372
  106.1 12.9 %all_to_all.21 = bf16[4,128,512]{2,1,0:T(8,128)(2,1)S(1)} all-to-all(bf16[4,128,512]{2,1,0:T(8,128)(2,1)S(1)} %bitcast.12), channel_id=1, replica_groups=mesh['z'=8,'y'=4,'c'=2,'x'=4] {'x'}, dimensions={0} | all-to-all | bytes 1048576 | tf_op jit(solution)/shard_map/all_to_all | solution.py:487
  119.2 7.6 %project.1 = bf16[128,4096]{1,0:T(8,128)(2,1)} custom-call(s32[5]{0:T(128)S(1)} %copy-done.16, bf16[128,2048]{1,0:T(8,128)(2,1)S(1)} %bitcast.13, bf16[512,4096]{1,0:T(8,128)(2,1)} %w0.1, bf16[256,4096]{1,0:T(8,128)(2,1)S(1)} %copy-done.2, bf16[256,4096]{1,0:T(8,128)(2,1)} %get-tuple-element.26.refs_1_, bf16[128,4096]{1,0:T(8,128)(2,1)S(1)} %get-tuple-element.29.refs_2_, ...), custom_call_target="tpu_custom_call" | custom-call | flops 1048576 | bytes 1048576 | tf_op jit(solution)/shard_map/project/pallas_call | solution.py:430
  (90 shorter events, 20.9 us)
Async XLA Ops:
  3.2 50.2 %collective-permute-start.15 = (bf16[256,4096]{1,0:T(8,128)(2,1)}, bf16[256,4096]{1,0:T(8,128)(2,1)S(1)}, u32[]{:S(2)}, u32[]{:S(2)}) collective-permute-start(bf16[256,4096]{1,0:T(8,128)(2,1)} %constant_dynamic-slice_fusion), channel_id=1, source_target_pairs={{0,1},{1,2},{2,3},{3,0},{4,5},{5,6},{6,7},{7,4},{8,9},{9,10},{10,1... | collective-permute-start | bytes 6291464 | tf_op jit(solution)/shard_map/ppermute | solution.py:447
  5.3 48.2 %collective-permute-start.16 = (bf16[256,4096]{1,0:T(8,128)(2,1)}, bf16[256,4096]{1,0:T(8,128)(2,1)}, u32[]{:S(2)}, u32[]{:S(2)}) collective-permute-start(bf16[256,4096]{1,0:T(8,128)(2,1)} %constant_dynamic-slice_fusion), channel_id=1, source_target_pairs={{0,3},{1,0},{2,1},{3,2},{4,7},{5,4},{6,5},{7,6},{8,11},{9,8},{10,9... | collective-permute-start | bytes 6291464 | tf_op jit(solution)/shard_map/ppermute | solution.py:447
  7.4 13.7 %all-to-all-start = ((bf16[8,80,256]{2,1,0:T(8,128)(2,1)}), bf16[8,80,256]{2,1,0:T(8,128)(2,1)S(1)}, u32[]{:S(2)}, u32[]{:S(2)}) async-start(bf16[8,80,256]{2,1,0:T(8,128)(2,1)} %get-tuple-element.20), calls=%async_computation | async-start | bytes 655360 | tf_op jit(solution)/shard_map/all_to_all | solution.py:455
  13.9 10.8 %collective-permute-start = (bf16[512,256]{1,0:T(8,128)(2,1)S(1)}, bf16[512,256]{1,0:T(8,128)(2,1)S(1)}, u32[]{:S(2)}, u32[]{:S(2)}) collective-permute-start(bf16[512,256]{1,0:T(8,128)(2,1)S(1)} %get-tuple-element.18), channel_id=1, source_target_pairs={{0,4},{4,8},{8,12},{12,16},{16,20},{20,24},{24,28},{28,32},{32,36}... | collective-permute-start | bytes 786440 | tf_op jit(solution)/shard_map/ppermute | solution.py:469
  21.1 8.6 %collective-permute-start.1 = (bf16[272,256]{1,0:T(8,128)(2,1)S(1)}, bf16[272,256]{1,0:T(8,128)(2,1)S(1)}, u32[]{:S(2)}, u32[]{:S(2)}) collective-permute-start(bf16[272,256]{1,0:T(8,128)(2,1)S(1)} %get-tuple-element.21.refs_0_), channel_id=1, source_target_pairs={{0,32},{32,64},{64,96},{96,128},{128,160},{160,192},{192,224},{224... | collective-permute-start | bytes 417800 | tf_op jit(solution)/shard_map/ppermute | solution.py:447
  23.0 9.3 %collective-permute-start.2 = (bf16[272,256]{1,0:T(8,128)(2,1)S(1)}, bf16[272,256]{1,0:T(8,128)(2,1)S(1)}, u32[]{:S(2)}, u32[]{:S(2)}) collective-permute-start(bf16[272,256]{1,0:T(8,128)(2,1)S(1)} %get-tuple-element.22.refs_1_), channel_id=1, source_target_pairs={{0,32},{32,64},{64,96},{96,128},{128,160},{160,192},{192,224},{224... | collective-permute-start | bytes 417800 | tf_op jit(solution)/shard_map/ppermute | solution.py:447
  24.7 7.6 %collective-permute-start.8 = (bf16[272,256]{1,0:T(8,128)(2,1)S(1)}, bf16[272,256]{1,0:T(8,128)(2,1)S(1)}, u32[]{:S(2)}, u32[]{:S(2)}) collective-permute-start(bf16[272,256]{1,0:T(8,128)(2,1)S(1)} %get-tuple-element.22.refs_1_), channel_id=1, source_target_pairs={{0,224},{32,0},{64,32},{96,64},{128,96},{160,128},{192,160},{224,1... | collective-permute-start | bytes 417800 | tf_op jit(solution)/shard_map/ppermute | solution.py:447
  29.7 4.3 %collective-permute-start.12 = (bf16[272,256]{1,0:T(8,128)(2,1)S(1)}, bf16[272,256]{1,0:T(8,128)(2,1)S(1)}, u32[]{:S(2)}, u32[]{:S(2)}) collective-permute-start(bf16[272,256]{1,0:T(8,128)(2,1)S(1)} %get-tuple-element.21.refs_0_), channel_id=1, source_target_pairs={{0,224},{32,0},{64,32},{96,64},{128,96},{160,128},{192,160},{224,1... | collective-permute-start | bytes 417800 | tf_op jit(solution)/shard_map/ppermute | solution.py:447
  32.3 5.4 %collective-permute-start.3 = (bf16[272,256]{1,0:T(8,128)(2,1)S(1)}, bf16[272,256]{1,0:T(8,128)(2,1)S(1)}, u32[]{:S(2)}, u32[]{:S(2)}) collective-permute-start(bf16[272,256]{1,0:T(8,128)(2,1)S(1)} %collective-permute-done.1.refs_2_), channel_id=1, source_target_pairs={{0,32},{32,64},{64,96},{96,128},{128,160},{160,192},{192,224},{224... | collective-permute-start | bytes 417800 | tf_op jit(solution)/shard_map/ppermute | solution.py:447
  32.3 6.9 %collective-permute-start.4 = (bf16[272,256]{1,0:T(8,128)(2,1)S(1)}, bf16[272,256]{1,0:T(8,128)(2,1)S(1)}, u32[]{:S(2)}, u32[]{:S(2)}) collective-permute-start(bf16[272,256]{1,0:T(8,128)(2,1)S(1)} %collective-permute-done.2.refs_3_), channel_id=1, source_target_pairs={{0,32},{32,64},{64,96},{96,128},{128,160},{160,192},{192,224},{224... | collective-permute-start | bytes 417800 | tf_op jit(solution)/shard_map/ppermute | solution.py:447
  34.0 5.3 %collective-permute-start.9 = (bf16[272,256]{1,0:T(8,128)(2,1)S(1)}, bf16[272,256]{1,0:T(8,128)(2,1)S(1)}, u32[]{:S(2)}, u32[]{:S(2)}) collective-permute-start(bf16[272,256]{1,0:T(8,128)(2,1)S(1)} %collective-permute-done.8.refs_15_), channel_id=1, source_target_pairs={{0,224},{32,0},{64,32},{96,64},{128,96},{160,128},{192,160},{224,1... | collective-permute-start | bytes 417800 | tf_op jit(solution)/shard_map/ppermute | solution.py:447
  39.2 5.4 %collective-permute-start.5 = (bf16[272,256]{1,0:T(8,128)(2,1)S(1)}, bf16[272,256]{1,0:T(8,128)(2,1)}, u32[]{:S(2)}, u32[]{:S(2)}) collective-permute-start(bf16[272,256]{1,0:T(8,128)(2,1)S(1)} %collective-permute-done.3.refs_4_), channel_id=1, source_target_pairs={{0,32},{32,64},{64,96},{96,128},{128,160},{160,192},{192,224},{224... | collective-permute-start | bytes 417800 | tf_op jit(solution)/shard_map/ppermute | solution.py:447
  39.4 6.7 %collective-permute-start.6 = (bf16[272,256]{1,0:T(8,128)(2,1)S(1)}, bf16[272,256]{1,0:T(8,128)(2,1)S(1)}, u32[]{:S(2)}, u32[]{:S(2)}) collective-permute-start(bf16[272,256]{1,0:T(8,128)(2,1)S(1)} %collective-permute-done.4.refs_5_), channel_id=1, source_target_pairs={{0,32},{32,64},{64,96},{96,128},{128,160},{160,192},{192,224},{224... | collective-permute-start | bytes 417800 | tf_op jit(solution)/shard_map/ppermute | solution.py:447
  42.0 5.4 %collective-permute-start.10 = (bf16[272,256]{1,0:T(8,128)(2,1)S(1)}, bf16[272,256]{1,0:T(8,128)(2,1)}, u32[]{:S(2)}, u32[]{:S(2)}) collective-permute-start(bf16[272,256]{1,0:T(8,128)(2,1)S(1)} %collective-permute-done.9.refs_13_), channel_id=1, source_target_pairs={{0,224},{32,0},{64,32},{96,64},{128,96},{160,128},{192,160},{224,1... | collective-permute-start | bytes 417800 | tf_op jit(solution)/shard_map/ppermute | solution.py:447
  44.6 6.4 %collective-permute-start.14 = (bf16[272,256]{1,0:T(8,128)(2,1)}, bf16[272,256]{1,0:T(8,128)(2,1)}, u32[]{:S(2)}, u32[]{:S(2)}) collective-permute-start(bf16[272,256]{1,0:T(8,128)(2,1)} %collective-permute-done.13.refs_12_), channel_id=1, source_target_pairs={{0,224},{32,0},{64,32},{96,64},{128,96},{160,128},{192,160},{224,1... | collective-permute-start | bytes 417800 | tf_op jit(solution)/shard_map/ppermute | solution.py:447
  46.1 5.6 %collective-permute-start.7 = (bf16[272,256]{1,0:T(8,128)(2,1)}, bf16[272,256]{1,0:T(8,128)(2,1)}, u32[]{:S(2)}, u32[]{:S(2)}) collective-permute-start(bf16[272,256]{1,0:T(8,128)(2,1)} %collective-permute-done.5.refs_6_), channel_id=1, source_target_pairs={{0,32},{32,64},{64,96},{96,128},{128,160},{160,192},{192,224},{224... | collective-permute-start | bytes 417800 | tf_op jit(solution)/shard_map/ppermute | solution.py:447
  47.4 6.1 %collective-permute-start.11 = (bf16[272,256]{1,0:T(8,128)(2,1)}, bf16[272,256]{1,0:T(8,128)(2,1)}, u32[]{:S(2)}, u32[]{:S(2)}) collective-permute-start(bf16[272,256]{1,0:T(8,128)(2,1)} %collective-permute-done.10.refs_11_), channel_id=1, source_target_pairs={{0,224},{32,0},{64,32},{96,64},{128,96},{160,128},{192,160},{224,1... | collective-permute-start | bytes 417800 | tf_op jit(solution)/shard_map/ppermute | solution.py:447
  60.7 30.9 %all-to-all-start.1 = ((bf16[8,384,256]{2,1,0:T(8,128)(2,1)}), bf16[8,384,256]{2,1,0:T(8,128)(2,1)}, u32[]{:S(2)}, u32[]{:S(2)}) async-start(bf16[8,384,256]{2,1,0:T(8,128)(2,1)} %bitcast.15), calls=%async_computation.1 | async-start | bytes 3145728 | tf_op jit(solution)/shard_map/all_to_all | solution.py:455
  70.7 33.8 %collective-permute-start.17 = (bf16[128,4096]{1,0:T(8,128)(2,1)}, bf16[128,4096]{1,0:T(8,128)(2,1)S(1)}, u32[]{:S(2)}, u32[]{:S(2)}) collective-permute-start(bf16[128,4096]{1,0:T(8,128)(2,1)} %get-tuple-element.27), channel_id=1, source_target_pairs={{0,1},{1,2},{2,3},{3,0},{4,5},{5,6},{6,7},{7,4},{8,9},{9,10},{10,1... | collective-permute-start | bytes 3145736 | tf_op jit(solution)/shard_map/ppermute | solution.py:447
  71.7 32.9 %collective-permute-start.18 = (bf16[128,4096]{1,0:T(8,128)(2,1)}, bf16[128,4096]{1,0:T(8,128)(2,1)}, u32[]{:S(2)}, u32[]{:S(2)}) collective-permute-start(bf16[128,4096]{1,0:T(8,128)(2,1)} %get-tuple-element.28), channel_id=1, source_target_pairs={{0,3},{1,0},{2,1},{3,2},{4,7},{5,4},{6,5},{7,6},{8,11},{9,8},{10,9... | collective-permute-start | bytes 3145736 | tf_op jit(solution)/shard_map/ppermute | solution.py:447
  73.4 45.7 %collective-permute-start.19 = (bf16[256,4096]{1,0:T(8,128)(2,1)S(1)}, bf16[256,4096]{1,0:T(8,128)(2,1)}, u32[]{:S(2)}, u32[]{:S(2)}) collective-permute-start(bf16[256,4096]{1,0:T(8,128)(2,1)S(1)} %copy-done.2), channel_id=1, source_target_pairs={{0,4},{4,0},{1,5},{5,1},{2,6},{6,2},{3,7},{7,3},{8,12},{12,8},{9,1... | collective-permute-start | bytes 6291464 | tf_op jit(solution)/shard_map/ppermute | solution.py:451
  74.2 45.0 %collective-permute-start.20 = (bf16[256,4096]{1,0:T(8,128)(2,1)}, bf16[256,4096]{1,0:T(8,128)(2,1)}, u32[]{:S(2)}, u32[]{:S(2)}) collective-permute-start(bf16[256,4096]{1,0:T(8,128)(2,1)} %get-tuple-element.26.refs_1_), channel_id=1, source_target_pairs={{0,4},{4,0},{1,5},{5,1},{2,6},{6,2},{3,7},{7,3},{8,12},{12,8},{9,1... | collective-permute-start | bytes 6291464 | tf_op jit(solution)/shard_map/ppermute | solution.py:451
  105.6 13.5 %collective-permute-start.21 = (bf16[128,4096]{1,0:T(8,128)(2,1)S(1)}, bf16[128,4096]{1,0:T(8,128)(2,1)S(1)}, u32[]{:S(2)}, u32[]{:S(2)}) collective-permute-start(bf16[128,4096]{1,0:T(8,128)(2,1)S(1)} %get-tuple-element.29.refs_2_), channel_id=1, source_target_pairs={{0,4},{4,0},{1,5},{5,1},{2,6},{6,2},{3,7},{7,3},{8,12},{12,8},{9,1... | collective-permute-start | bytes 3145736 | tf_op jit(solution)/shard_map/ppermute | solution.py:451
  105.6 13.5 %collective-permute-start.22 = (bf16[128,4096]{1,0:T(8,128)(2,1)}, bf16[128,4096]{1,0:T(8,128)(2,1)S(1)}, u32[]{:S(2)}, u32[]{:S(2)}) collective-permute-start(bf16[128,4096]{1,0:T(8,128)(2,1)} %get-tuple-element.30.refs_3_), channel_id=1, source_target_pairs={{0,4},{4,0},{1,5},{5,1},{2,6},{6,2},{3,7},{7,3},{8,12},{12,8},{9,1... | collective-permute-start | bytes 3145736 | tf_op jit(solution)/shard_map/ppermute | solution.py:451
  (26 other events, 362.9 us)

commit v3 on v2

--- a/solution.py
+++ b/solution.py
@@ -93,8 +93,11 @@
         act(refs[0])
         return
     half = len(refs) // 2
-    pl.when(index < half)(lambda: choose(refs[:half], index, act))
-    pl.when(index >= half)(lambda: choose(refs[half:], index - half, act))
+    lax.cond(
+        index < half,
+        lambda: choose(refs[:half], index, act),
+        lambda: choose(refs[half:], index - half, act),
+    )
 
 
 def pick_kernel(place_ref, picks_ref, *refs):
@@ -123,7 +126,7 @@
 
     for copy in sides:
         copy.start()
-    lax.fori_loop(0, PIECES * PICKS, step, 0, unroll=4)
+    lax.fori_loop(0, PIECES * PICKS, step, 0, unroll=8)
     pltpu.make_async_copy(out, out, sem).wait()
     for copy in sides:
         copy.wait()

time: 127 us -> 127 us (level)
  no operation moved by 1% of the time
where the time goes in v3:
time: 127 us
  starting transfers between devices  43 us (34%)
  Pallas kernels  34.7 us (27%)
  waiting for transfers between devices  24.6 us (19%)
  blocking collectives  12.9 us (10%)
  local copies, waits for them, and re-layouts  11.1 us (9%)
    ppermute x18, starting transfers between devices, shift(): return lax.ppermute(x, axis, [(i, (i + by) % size) for i in range(size)])  21.7 us
    all_to_all x2, starting transfers between devices, to_plane(): return lax.all_to_all(x, ('y', 'c'), 0, 0, tiled=True)  16.5 us
    ppermute x18, waiting for transfers between devices, shift(): return lax.ppermute(x, axis, [(i, (i + by) % size) for i in range(size)])  15.2 us
    pallas_call x1, Pallas kernels, far_attention(): pl.pallas_call(far_kernel, grid_spec=pltpu.PrefetchScalarGridSpec(num_sca...  13 us
    all_to_all x1, blocking collectives, per_device(): lax.all_to_all(attended.reshape(NX, TILE, QPK * HD), 'x', 0, 0, tiled=True)  12.9 us
    all_to_all x2, waiting for transfers between devices, to_plane(): return lax.all_to_all(x, ('y', 'c'), 0, 0, tiled=True)  9.39 us
    pallas_call x1, Pallas kernels, project(): pl.pallas_call(project_kernel, grid_spec=pltpu.PrefetchScalarGridSpec(num...  7.56 us
    unnamed x51, local copies, waits for them, and re-layouts  7.2 us
  transfers between devices with their start and end apart: 25, of which 14 were waited for; matrix products, arithmetic and copies ran while one was open for 1% of the time, Pallas kernels for 17%

profile of v3, /device:TPU:1, one launch (start us, length us, event | category | flops | bytes accessed | tf_op | source)
XLA Modules:
  0.0 126.6 jit_solution(15374400137420218237)
XLA Ops:
  0.0 3.2 %constant_dynamic-slice_fusion = bf16[256,4096]{1,0:T(8,128)(2,1)} fusion(bf16[512,4096]{1,0:T(8,128)(2,1)} %w0.1, s32[]{:T(128)S(6)} %select_n.7), kind=kLoop, calls=%fused_computation | loop fusion | bytes 4194308 | tf_op jit(solution)/shard_map/dynamic_slice | solution.py:466
  3.2 2.0 %collective-permute-start.15 = (bf16[256,4096]{1,0:T(8,128)(2,1)}, bf16[256,4096]{1,0:T(8,128)(2,1)S(1)}, u32[]{:S(2)}, u32[]{:S(2)}) collective-permute-start(bf16[256,4096]{1,0:T(8,128)(2,1)} %constant_dynamic-slice_fusion), channel_id=1, source_target_pairs={{0,1},{1,2},{2,3},{3,0},{4,5},{5,6},{6,7},{7,4},{8,9},{9,10},{10,1... | collective-permute-start | bytes 6291464 | tf_op jit(solution)/shard_map/ppermute | solution.py:450
  7.4 6.5 %all-to-all-start = ((bf16[8,80,256]{2,1,0:T(8,128)(2,1)}), bf16[8,80,256]{2,1,0:T(8,128)(2,1)S(1)}, u32[]{:S(2)}, u32[]{:S(2)}) async-start(bf16[8,80,256]{2,1,0:T(8,128)(2,1)} %get-tuple-element.20), calls=%async_computation | async-start | bytes 655360 | tf_op jit(solution)/shard_map/all_to_all | solution.py:458
  13.9 3.5 %collective-permute-start = (bf16[512,256]{1,0:T(8,128)(2,1)S(1)}, bf16[512,256]{1,0:T(8,128)(2,1)S(1)}, u32[]{:S(2)}, u32[]{:S(2)}) collective-permute-start(bf16[512,256]{1,0:T(8,128)(2,1)S(1)} %get-tuple-element.18), channel_id=1, source_target_pairs={{0,4},{4,8},{8,12},{12,16},{16,20},{20,24},{24,28},{28,32},{32,36}... | collective-permute-start | bytes 786440 | tf_op jit(solution)/shard_map/ppermute | solution.py:472
  17.4 3.6 %all-to-all-done.msg_ref = bf16[8,80,256]{2,1,0:T(8,128)(2,1)S(1)} async-done(((bf16[8,80,256]{2,1,0:T(8,128)(2,1)}), bf16[8,80,256]{2,1,0:T(8,128)(2,1)S(1)}, u32[]{:S(2)}, u32[]{:S(2)}) %all-to-all-start) | async-done | bytes 327712 | tf_op jit(solution)/shard_map/all_to_all | solution.py:458
  21.1 1.9 %collective-permute-start.1 = (bf16[272,256]{1,0:T(8,128)(2,1)S(1)}, bf16[272,256]{1,0:T(8,128)(2,1)S(1)}, u32[]{:S(2)}, u32[]{:S(2)}) collective-permute-start(bf16[272,256]{1,0:T(8,128)(2,1)S(1)} %get-tuple-element.21.refs_0_), channel_id=1, source_target_pairs={{0,32},{32,64},{64,96},{96,128},{128,160},{160,192},{192,224},{224... | collective-permute-start | bytes 417800 | tf_op jit(solution)/shard_map/ppermute | solution.py:450
  23.0 1.6 %collective-permute-start.2 = (bf16[272,256]{1,0:T(8,128)(2,1)S(1)}, bf16[272,256]{1,0:T(8,128)(2,1)S(1)}, u32[]{:S(2)}, u32[]{:S(2)}) collective-permute-start(bf16[272,256]{1,0:T(8,128)(2,1)S(1)} %get-tuple-element.22.refs_1_), channel_id=1, source_target_pairs={{0,32},{32,64},{64,96},{96,128},{128,160},{160,192},{192,224},{224... | collective-permute-start | bytes 417800 | tf_op jit(solution)/shard_map/ppermute | solution.py:450
  24.7 2.5 %collective-permute-start.8 = (bf16[272,256]{1,0:T(8,128)(2,1)S(1)}, bf16[272,256]{1,0:T(8,128)(2,1)S(1)}, u32[]{:S(2)}, u32[]{:S(2)}) collective-permute-start(bf16[272,256]{1,0:T(8,128)(2,1)S(1)} %get-tuple-element.22.refs_1_), channel_id=1, source_target_pairs={{0,224},{32,0},{64,32},{96,64},{128,96},{160,128},{192,160},{224,1... | collective-permute-start | bytes 417800 | tf_op jit(solution)/shard_map/ppermute | solution.py:450
  27.2 2.5 %collective-permute-done.1.refs_2_ = bf16[272,256]{1,0:T(8,128)(2,1)S(1)} collective-permute-done((bf16[272,256]{1,0:T(8,128)(2,1)S(1)}, bf16[272,256]{1,0:T(8,128)(2,1)S(1)}, u32[]{:S(2)}, u32[]{:S(2)}) %collective-permute-start.1) | collective-permute-done | bytes 139296 | tf_op jit(solution)/shard_map/ppermute | solution.py:450
  32.4 1.6 %collective-permute-done.12.refs_14_ = bf16[272,256]{1,0:T(8,128)(2,1)S(1)} collective-permute-done((bf16[272,256]{1,0:T(8,128)(2,1)S(1)}, bf16[272,256]{1,0:T(8,128)(2,1)S(1)}, u32[]{:S(2)}, u32[]{:S(2)}) %collective-permute-start.12) | collective-permute-done | bytes 139296 | tf_op jit(solution)/shard_map/ppermute | solution.py:450
  34.0 3.3 %collective-permute-start.9 = (bf16[272,256]{1,0:T(8,128)(2,1)S(1)}, bf16[272,256]{1,0:T(8,128)(2,1)S(1)}, u32[]{:S(2)}, u32[]{:S(2)}) collective-permute-start(bf16[272,256]{1,0:T(8,128)(2,1)S(1)} %collective-permute-done.8.refs_15_), channel_id=1, source_target_pairs={{0,224},{32,0},{64,32},{96,64},{128,96},{160,128},{192,160},{224,1... | collective-permute-start | bytes 417800 | tf_op jit(solution)/shard_map/ppermute | solution.py:450
  39.4 2.7 %collective-permute-done.13.refs_12_ = bf16[272,256]{1,0:T(8,128)(2,1)} collective-permute-done((bf16[272,256]{1,0:T(8,128)(2,1)S(1)}, bf16[272,256]{1,0:T(8,128)(2,1)}, u32[]{:S(2)}, u32[]{:S(2)}) %collective-permute-start.13) | collective-permute-done | bytes 139296 | tf_op jit(solution)/shard_map/ppermute | solution.py:450
  42.0 2.2 %collective-permute-start.10 = (bf16[272,256]{1,0:T(8,128)(2,1)S(1)}, bf16[272,256]{1,0:T(8,128)(2,1)}, u32[]{:S(2)}, u32[]{:S(2)}) collective-permute-start(bf16[272,256]{1,0:T(8,128)(2,1)S(1)} %collective-permute-done.9.refs_13_), channel_id=1, source_target_pairs={{0,224},{32,0},{64,32},{96,64},{128,96},{160,128},{192,160},{224,1... | collective-permute-start | bytes 417800 | tf_op jit(solution)/shard_map/ppermute | solution.py:450
  47.4 2.3 %collective-permute-start.11 = (bf16[272,256]{1,0:T(8,128)(2,1)}, bf16[272,256]{1,0:T(8,128)(2,1)}, u32[]{:S(2)}, u32[]{:S(2)}) collective-permute-start(bf16[272,256]{1,0:T(8,128)(2,1)} %collective-permute-done.10.refs_11_), channel_id=1, source_target_pairs={{0,224},{32,0},{64,32},{96,64},{128,96},{160,128},{192,160},{224,1... | collective-permute-start | bytes 417800 | tf_op jit(solution)/shard_map/ppermute | solution.py:450
  51.7 1.7 %collective-permute-done.11.refs_9_ = bf16[272,256]{1,0:T(8,128)(2,1)} collective-permute-done((bf16[272,256]{1,0:T(8,128)(2,1)}, bf16[272,256]{1,0:T(8,128)(2,1)}, u32[]{:S(2)}, u32[]{:S(2)}) %collective-permute-start.11) | collective-permute-done | bytes 139296 | tf_op jit(solution)/shard_map/ppermute | solution.py:450
  54.8 5.8 %pick_pieces.1 = (bf16[256,4096]{1,0:T(8,128)(2,1)}, bf16[256,4096]{1,0:T(8,128)(2,1)}, bf16[3072,256]{1,0:T(8,128)(2,1)}, bf16[128,4096]{1,0:T(8,128)(2,1)}, bf16[128,4096]{1,0:T(8,128)(2,1)}) custom-call(s32[5]{0:T(128)} %stack.23.place_ref, s32[8,7]{1,0:T(8,128)} %bitcast.16, ...), custom_call_target="tpu_custom_call", output_to_operand_aliasing={{0}: (19, {}), {1}: (20, {})} | custom-call | bytes 1048576 | tf_op jit(solution)/shard_map/pick_pieces/pallas_call | solution.py:140
  60.6 10.0 %all-to-all-start.1 = ((bf16[8,384,256]{2,1,0:T(8,128)(2,1)}), bf16[8,384,256]{2,1,0:T(8,128)(2,1)}, u32[]{:S(2)}, u32[]{:S(2)}) async-start(bf16[8,384,256]{2,1,0:T(8,128)(2,1)} %bitcast.15), calls=%async_computation.1 | async-start | bytes 3145728 | tf_op jit(solution)/shard_map/all_to_all | solution.py:458
  71.6 1.7 %collective-permute-start.18 = (bf16[128,4096]{1,0:T(8,128)(2,1)}, bf16[128,4096]{1,0:T(8,128)(2,1)}, u32[]{:S(2)}, u32[]{:S(2)}) collective-permute-start(bf16[128,4096]{1,0:T(8,128)(2,1)} %get-tuple-element.28), channel_id=1, source_target_pairs={{0,3},{1,0},{2,1},{3,2},{4,7},{5,4},{6,5},{7,6},{8,11},{9,8},{10,9... | collective-permute-start | bytes 3145736 | tf_op jit(solution)/shard_map/ppermute | solution.py:450
  76.1 3.7 %near_attention.1 = (bf16[2048,128]{1,0:T(8,128)(2,1)S(1)}, f32[2048,256]{1,0:T(8,128)S(1)}) custom-call(s32[5]{0:T(128)S(1)} %copy-done.15, bf16[512,512]{1,0:T(8,128)(2,1)S(1)} %copy-done.10, bf16[512,128]{1,0:T(8,128)(2,1)S(1)} %copy-done.12, bf16[512,128]{1,0:T(8,128)(2,1)S(1)} %copy-done.14, bf16[512,256]{1,0:T(8,128)(2,1)S(1)} %copy-done.7), custom_call_target="tpu_custom_call" | custom-call | flops 1048576 | bytes 1048576 | tf_op jit(solution)/shard_map/near_attention/pallas_call | solution.py:208
  81.9 3.8 %summary_attention.1.summary_hbm = f32[2048,128]{1,0:T(8,128)} custom-call(s32[5]{0:T(128)} %stack.23.place_ref, bf16[2048,128]{1,0:T(8,128)(2,1)} %copy-done.5, bf16[272,256]{1,0:T(8,128)(2,1)} %copy-done.8, bf16[272,256]{1,0:T(8,128)(2,1)} %copy-done.9, bf16[272,256]{1,0:T(8,128)(2,1)} %copy-done.17, bf16[272,256]{1,0:T(8,128)(2,1)} %copy-done.18, ...), custom_call_target="tpu_custom_call" | custom-call | flops 1048576 | bytes 1048576 | tf_op jit(solution)/shard_map/summary_attention/pallas_call | solution.py:266
  85.7 5.8 %all-to-all-done.1 = bf16[8,384,256]{2,1,0:T(8,128)(2,1)} async-done(((bf16[8,384,256]{2,1,0:T(8,128)(2,1)}), bf16[8,384,256]{2,1,0:T(8,128)(2,1)}, u32[]{:S(2)}, u32[]{:S(2)}) %all-to-all-start.1) | async-done | bytes 1572896 | tf_op jit(solution)/shard_map/all_to_all | solution.py:458
  91.5 13.0 %far_attention.1.after_ref = bf16[512,512]{1,0:T(8,128)(2,1)} custom-call(s32[5]{0:T(128)} %stack.23.place_ref, s32[8,7]{1,0:T(8,128)} %bitcast.17, bf16[2048,128]{1,0:T(8,128)(2,1)} %copy-done.5, bf16[3072,256]{1,0:T(8,128)(2,1)} %bitcast.7.pieces_ref, f32[2048,256]{1,0:T(8,128)} %copy-done.4, f32[2048,128]{1,0:T(8,128)} %summary_attention.1.summary_hbm), custom_call_target="tpu_custom_call" | custom-call | flops 1048576 | bytes 1048576 | tf_op jit(solution)/shard_map/far_attention/pallas_call | solution.py:375
  106.1 12.9 %all_to_all.21 = bf16[4,128,512]{2,1,0:T(8,128)(2,1)S(1)} all-to-all(bf16[4,128,512]{2,1,0:T(8,128)(2,1)S(1)} %bitcast.12), channel_id=1, replica_groups=mesh['z'=8,'y'=4,'c'=2,'x'=4] {'x'}, dimensions={0} | all-to-all | bytes 1048576 | tf_op jit(solution)/shard_map/all_to_all | solution.py:490
  119.1 7.6 %project.1 = bf16[128,4096]{1,0:T(8,128)(2,1)} custom-call(s32[5]{0:T(128)S(1)} %copy-done.16, bf16[128,2048]{1,0:T(8,128)(2,1)S(1)} %bitcast.13, bf16[512,4096]{1,0:T(8,128)(2,1)} %w0.1, bf16[256,4096]{1,0:T(8,128)(2,1)S(1)} %copy-done.2, bf16[256,4096]{1,0:T(8,128)(2,1)} %get-tuple-element.26.refs_1_, bf16[128,4096]{1,0:T(8,128)(2,1)S(1)} %get-tuple-element.29.refs_2_, ...), custom_call_target="tpu_custom_call" | custom-call | flops 1048576 | bytes 1048576 | tf_op jit(solution)/shard_map/project/pallas_call | solution.py:433
  (90 shorter events, 20.9 us)
Async XLA Ops:
  3.2 50.2 %collective-permute-start.15 = (bf16[256,4096]{1,0:T(8,128)(2,1)}, bf16[256,4096]{1,0:T(8,128)(2,1)S(1)}, u32[]{:S(2)}, u32[]{:S(2)}) collective-permute-start(bf16[256,4096]{1,0:T(8,128)(2,1)} %constant_dynamic-slice_fusion), channel_id=1, source_target_pairs={{0,1},{1,2},{2,3},{3,0},{4,5},{5,6},{6,7},{7,4},{8,9},{9,10},{10,1... | collective-permute-start | bytes 6291464 | tf_op jit(solution)/shard_map/ppermute | solution.py:450
  5.3 48.2 %collective-permute-start.16 = (bf16[256,4096]{1,0:T(8,128)(2,1)}, bf16[256,4096]{1,0:T(8,128)(2,1)}, u32[]{:S(2)}, u32[]{:S(2)}) collective-permute-start(bf16[256,4096]{1,0:T(8,128)(2,1)} %constant_dynamic-slice_fusion), channel_id=1, source_target_pairs={{0,3},{1,0},{2,1},{3,2},{4,7},{5,4},{6,5},{7,6},{8,11},{9,8},{10,9... | collective-permute-start | bytes 6291464 | tf_op jit(solution)/shard_map/ppermute | solution.py:450
  7.4 13.7 %all-to-all-start = ((bf16[8,80,256]{2,1,0:T(8,128)(2,1)}), bf16[8,80,256]{2,1,0:T(8,128)(2,1)S(1)}, u32[]{:S(2)}, u32[]{:S(2)}) async-start(bf16[8,80,256]{2,1,0:T(8,128)(2,1)} %get-tuple-element.20), calls=%async_computation | async-start | bytes 655360 | tf_op jit(solution)/shard_map/all_to_all | solution.py:458
  13.9 10.8 %collective-permute-start = (bf16[512,256]{1,0:T(8,128)(2,1)S(1)}, bf16[512,256]{1,0:T(8,128)(2,1)S(1)}, u32[]{:S(2)}, u32[]{:S(2)}) collective-permute-start(bf16[512,256]{1,0:T(8,128)(2,1)S(1)} %get-tuple-element.18), channel_id=1, source_target_pairs={{0,4},{4,8},{8,12},{12,16},{16,20},{20,24},{24,28},{28,32},{32,36}... | collective-permute-start | bytes 786440 | tf_op jit(solution)/shard_map/ppermute | solution.py:472
  21.1 8.6 %collective-permute-start.1 = (bf16[272,256]{1,0:T(8,128)(2,1)S(1)}, bf16[272,256]{1,0:T(8,128)(2,1)S(1)}, u32[]{:S(2)}, u32[]{:S(2)}) collective-permute-start(bf16[272,256]{1,0:T(8,128)(2,1)S(1)} %get-tuple-element.21.refs_0_), channel_id=1, source_target_pairs={{0,32},{32,64},{64,96},{96,128},{128,160},{160,192},{192,224},{224... | collective-permute-start | bytes 417800 | tf_op jit(solution)/shard_map/ppermute | solution.py:450
  23.0 9.3 %collective-permute-start.2 = (bf16[272,256]{1,0:T(8,128)(2,1)S(1)}, bf16[272,256]{1,0:T(8,128)(2,1)S(1)}, u32[]{:S(2)}, u32[]{:S(2)}) collective-permute-start(bf16[272,256]{1,0:T(8,128)(2,1)S(1)} %get-tuple-element.22.refs_1_), channel_id=1, source_target_pairs={{0,32},{32,64},{64,96},{96,128},{128,160},{160,192},{192,224},{224... | collective-permute-start | bytes 417800 | tf_op jit(solution)/shard_map/ppermute | solution.py:450
  24.7 7.6 %collective-permute-start.8 = (bf16[272,256]{1,0:T(8,128)(2,1)S(1)}, bf16[272,256]{1,0:T(8,128)(2,1)S(1)}, u32[]{:S(2)}, u32[]{:S(2)}) collective-permute-start(bf16[272,256]{1,0:T(8,128)(2,1)S(1)} %get-tuple-element.22.refs_1_), channel_id=1, source_target_pairs={{0,224},{32,0},{64,32},{96,64},{128,96},{160,128},{192,160},{224,1... | collective-permute-start | bytes 417800 | tf_op jit(solution)/shard_map/ppermute | solution.py:450
  29.7 4.3 %collective-permute-start.12 = (bf16[272,256]{1,0:T(8,128)(2,1)S(1)}, bf16[272,256]{1,0:T(8,128)(2,1)S(1)}, u32[]{:S(2)}, u32[]{:S(2)}) collective-permute-start(bf16[272,256]{1,0:T(8,128)(2,1)S(1)} %get-tuple-element.21.refs_0_), channel_id=1, source_target_pairs={{0,224},{32,0},{64,32},{96,64},{128,96},{160,128},{192,160},{224,1... | collective-permute-start | bytes 417800 | tf_op jit(solution)/shard_map/ppermute | solution.py:450
  32.3 5.4 %collective-permute-start.3 = (bf16[272,256]{1,0:T(8,128)(2,1)S(1)}, bf16[272,256]{1,0:T(8,128)(2,1)S(1)}, u32[]{:S(2)}, u32[]{:S(2)}) collective-permute-start(bf16[272,256]{1,0:T(8,128)(2,1)S(1)} %collective-permute-done.1.refs_2_), channel_id=1, source_target_pairs={{0,32},{32,64},{64,96},{96,128},{128,160},{160,192},{192,224},{224... | collective-permute-start | bytes 417800 | tf_op jit(solution)/shard_map/ppermute | solution.py:450
  32.3 6.9 %collective-permute-start.4 = (bf16[272,256]{1,0:T(8,128)(2,1)S(1)}, bf16[272,256]{1,0:T(8,128)(2,1)S(1)}, u32[]{:S(2)}, u32[]{:S(2)}) collective-permute-start(bf16[272,256]{1,0:T(8,128)(2,1)S(1)} %collective-permute-done.2.refs_3_), channel_id=1, source_target_pairs={{0,32},{32,64},{64,96},{96,128},{128,160},{160,192},{192,224},{224... | collective-permute-start | bytes 417800 | tf_op jit(solution)/shard_map/ppermute | solution.py:450
  34.0 5.3 %collective-permute-start.9 = (bf16[272,256]{1,0:T(8,128)(2,1)S(1)}, bf16[272,256]{1,0:T(8,128)(2,1)S(1)}, u32[]{:S(2)}, u32[]{:S(2)}) collective-permute-start(bf16[272,256]{1,0:T(8,128)(2,1)S(1)} %collective-permute-done.8.refs_15_), channel_id=1, source_target_pairs={{0,224},{32,0},{64,32},{96,64},{128,96},{160,128},{192,160},{224,1... | collective-permute-start | bytes 417800 | tf_op jit(solution)/shard_map/ppermute | solution.py:450
  39.2 5.4 %collective-permute-start.5 = (bf16[272,256]{1,0:T(8,128)(2,1)S(1)}, bf16[272,256]{1,0:T(8,128)(2,1)}, u32[]{:S(2)}, u32[]{:S(2)}) collective-permute-start(bf16[272,256]{1,0:T(8,128)(2,1)S(1)} %collective-permute-done.3.refs_4_), channel_id=1, source_target_pairs={{0,32},{32,64},{64,96},{96,128},{128,160},{160,192},{192,224},{224... | collective-permute-start | bytes 417800 | tf_op jit(solution)/shard_map/ppermute | solution.py:450
  39.4 6.7 %collective-permute-start.6 = (bf16[272,256]{1,0:T(8,128)(2,1)S(1)}, bf16[272,256]{1,0:T(8,128)(2,1)S(1)}, u32[]{:S(2)}, u32[]{:S(2)}) collective-permute-start(bf16[272,256]{1,0:T(8,128)(2,1)S(1)} %collective-permute-done.4.refs_5_), channel_id=1, source_target_pairs={{0,32},{32,64},{64,96},{96,128},{128,160},{160,192},{192,224},{224... | collective-permute-start | bytes 417800 | tf_op jit(solution)/shard_map/ppermute | solution.py:450
  42.0 5.4 %collective-permute-start.10 = (bf16[272,256]{1,0:T(8,128)(2,1)S(1)}, bf16[272,256]{1,0:T(8,128)(2,1)}, u32[]{:S(2)}, u32[]{:S(2)}) collective-permute-start(bf16[272,256]{1,0:T(8,128)(2,1)S(1)} %collective-permute-done.9.refs_13_), channel_id=1, source_target_pairs={{0,224},{32,0},{64,32},{96,64},{128,96},{160,128},{192,160},{224,1... | collective-permute-start | bytes 417800 | tf_op jit(solution)/shard_map/ppermute | solution.py:450
  44.6 6.4 %collective-permute-start.14 = (bf16[272,256]{1,0:T(8,128)(2,1)}, bf16[272,256]{1,0:T(8,128)(2,1)}, u32[]{:S(2)}, u32[]{:S(2)}) collective-permute-start(bf16[272,256]{1,0:T(8,128)(2,1)} %collective-permute-done.13.refs_12_), channel_id=1, source_target_pairs={{0,224},{32,0},{64,32},{96,64},{128,96},{160,128},{192,160},{224,1... | collective-permute-start | bytes 417800 | tf_op jit(solution)/shard_map/ppermute | solution.py:450
  46.1 5.6 %collective-permute-start.7 = (bf16[272,256]{1,0:T(8,128)(2,1)}, bf16[272,256]{1,0:T(8,128)(2,1)}, u32[]{:S(2)}, u32[]{:S(2)}) collective-permute-start(bf16[272,256]{1,0:T(8,128)(2,1)} %collective-permute-done.5.refs_6_), channel_id=1, source_target_pairs={{0,32},{32,64},{64,96},{96,128},{128,160},{160,192},{192,224},{224... | collective-permute-start | bytes 417800 | tf_op jit(solution)/shard_map/ppermute | solution.py:450
  47.4 6.1 %collective-permute-start.11 = (bf16[272,256]{1,0:T(8,128)(2,1)}, bf16[272,256]{1,0:T(8,128)(2,1)}, u32[]{:S(2)}, u32[]{:S(2)}) collective-permute-start(bf16[272,256]{1,0:T(8,128)(2,1)} %collective-permute-done.10.refs_11_), channel_id=1, source_target_pairs={{0,224},{32,0},{64,32},{96,64},{128,96},{160,128},{192,160},{224,1... | collective-permute-start | bytes 417800 | tf_op jit(solution)/shard_map/ppermute | solution.py:450
  60.6 30.9 %all-to-all-start.1 = ((bf16[8,384,256]{2,1,0:T(8,128)(2,1)}), bf16[8,384,256]{2,1,0:T(8,128)(2,1)}, u32[]{:S(2)}, u32[]{:S(2)}) async-start(bf16[8,384,256]{2,1,0:T(8,128)(2,1)} %bitcast.15), calls=%async_computation.1 | async-start | bytes 3145728 | tf_op jit(solution)/shard_map/all_to_all | solution.py:458
  70.7 33.8 %collective-permute-start.17 = (bf16[128,4096]{1,0:T(8,128)(2,1)}, bf16[128,4096]{1,0:T(8,128)(2,1)S(1)}, u32[]{:S(2)}, u32[]{:S(2)}) collective-permute-start(bf16[128,4096]{1,0:T(8,128)(2,1)} %get-tuple-element.27), channel_id=1, source_target_pairs={{0,1},{1,2},{2,3},{3,0},{4,5},{5,6},{6,7},{7,4},{8,9},{9,10},{10,1... | collective-permute-start | bytes 3145736 | tf_op jit(solution)/shard_map/ppermute | solution.py:450
  71.6 32.9 %collective-permute-start.18 = (bf16[128,4096]{1,0:T(8,128)(2,1)}, bf16[128,4096]{1,0:T(8,128)(2,1)}, u32[]{:S(2)}, u32[]{:S(2)}) collective-permute-start(bf16[128,4096]{1,0:T(8,128)(2,1)} %get-tuple-element.28), channel_id=1, source_target_pairs={{0,3},{1,0},{2,1},{3,2},{4,7},{5,4},{6,5},{7,6},{8,11},{9,8},{10,9... | collective-permute-start | bytes 3145736 | tf_op jit(solution)/shard_map/ppermute | solution.py:450
  73.3 45.7 %collective-permute-start.19 = (bf16[256,4096]{1,0:T(8,128)(2,1)S(1)}, bf16[256,4096]{1,0:T(8,128)(2,1)}, u32[]{:S(2)}, u32[]{:S(2)}) collective-permute-start(bf16[256,4096]{1,0:T(8,128)(2,1)S(1)} %copy-done.2), channel_id=1, source_target_pairs={{0,4},{4,0},{1,5},{5,1},{2,6},{6,2},{3,7},{7,3},{8,12},{12,8},{9,1... | collective-permute-start | bytes 6291464 | tf_op jit(solution)/shard_map/ppermute | solution.py:454
  74.1 44.9 %collective-permute-start.20 = (bf16[256,4096]{1,0:T(8,128)(2,1)}, bf16[256,4096]{1,0:T(8,128)(2,1)}, u32[]{:S(2)}, u32[]{:S(2)}) collective-permute-start(bf16[256,4096]{1,0:T(8,128)(2,1)} %get-tuple-element.26.refs_1_), channel_id=1, source_target_pairs={{0,4},{4,0},{1,5},{5,1},{2,6},{6,2},{3,7},{7,3},{8,12},{12,8},{9,1... | collective-permute-start | bytes 6291464 | tf_op jit(solution)/shard_map/ppermute | solution.py:454
  105.6 13.5 %collective-permute-start.21 = (bf16[128,4096]{1,0:T(8,128)(2,1)S(1)}, bf16[128,4096]{1,0:T(8,128)(2,1)S(1)}, u32[]{:S(2)}, u32[]{:S(2)}) collective-permute-start(bf16[128,4096]{1,0:T(8,128)(2,1)S(1)} %get-tuple-element.29.refs_2_), channel_id=1, source_target_pairs={{0,4},{4,0},{1,5},{5,1},{2,6},{6,2},{3,7},{7,3},{8,12},{12,8},{9,1... | collective-permute-start | bytes 3145736 | tf_op jit(solution)/shard_map/ppermute | solution.py:454
  105.6 13.5 %collective-permute-start.22 = (bf16[128,4096]{1,0:T(8,128)(2,1)}, bf16[128,4096]{1,0:T(8,128)(2,1)S(1)}, u32[]{:S(2)}, u32[]{:S(2)}) collective-permute-start(bf16[128,4096]{1,0:T(8,128)(2,1)} %get-tuple-element.30.refs_3_), channel_id=1, source_target_pairs={{0,4},{4,0},{1,5},{5,1},{2,6},{6,2},{3,7},{7,3},{8,12},{12,8},{9,1... | collective-permute-start | bytes 3145736 | tf_op jit(solution)/shard_map/ppermute | solution.py:454
  (26 other events, 362.8 us)
